TPU v7x, 512 devices: a whole 4x8x8 slice. The times are simulated.
512 devices in a mesh: grp: 16 (over y, core), dev: 32 (over x, z).
Axes of the slice: x: 4, y: 8, z: 8, core: 2. Of those that a mesh axis runs over, the one named last changes fastest.
Arguments:
- forcing: float32 [8, 8, 8, 32, 16, 128], P(None, None, None, 'dev', 'grp'), may hold values from -6 to 6
- coefficient: float32 [32, 16, 128], P('dev', 'grp'), may hold values from 1 to 10
- coarse_inverse: float32 [16384, 1024], P(('grp', 'dev')), as said below
Outputs:
- solution: float32 [8, 8, 8, 32, 16, 128], P(None, None, None, 'dev', 'grp')
- residual: float32 [8, 8, 8, 32, 16, 128], P(None, None, None, 'dev', 'grp')
Inputs may be any that keep to these rules, and one draw needn't show every extreme that they name: Each group's block of coarse_inverse is symmetric and positive definite.
All inputs are finite; a program needn't handle non-finite values.
Results may differ from a plain program's by a relative error of at most 0.017.
Values sent between devices are 32-bit elements; how exact they have to be, the bound alone decides.
A program may use at most 64 MiB of HBM per device.

v0:
```python
import math

import jax
import jax.numpy as jnp
from jax import lax
from jax.sharding import PartitionSpec as P

NP = 8
ITERS = 2


HIGHEST = lax.Precision.HIGHEST
MASS_SHIFT = 0.1


def extended_2(x, sides, width, wrap):
    for axis, dim in sides:
        size, length = (lax.axis_size(axis), x.shape[dim])
        up = [(i, (i + 1) % size) for i in range(size if wrap else size - 1)]
        down = [(j, i) for i, j in up]
        last = lax.slice_in_dim(x, length - width, length, axis=dim)
        leading = lax.slice_in_dim(x, 0, width, axis=dim)
        before = lax.ppermute(last, axis, up)
        after = lax.ppermute(leading, axis, down)
        x = jnp.concatenate([before, x, after], axis=dim)
    return x


def legendre_pair(order, point):
    before = 1.0
    current = point
    for degree in range(2, order + 1):
        before, current = (
            current,
            ((2 * degree - 1) * point * current - (degree - 1) * before) / degree,
        )
    return (before, current)


def jacobi_eigen(matrix_in):
    count = len(matrix_in)
    work = [list(row_vals) for row_vals in matrix_in]
    vectors = [
        [1.0 if row_id == col_id else 0.0 for col_id in range(count)] for row_id in range(count)
    ]
    for sweep_id in range(14):
        for first_id in range(count - 1):
            for second_id in range(first_id + 1, count):
                off_value = work[first_id][second_id]
                if abs(off_value) > 1e-300:
                    theta = (work[second_id][second_id] - work[first_id][first_id]) / (
                        2.0 * off_value
                    )
                    sign_val = 1.0 if theta >= 0.0 else -1.0
                    tangent = sign_val / (abs(theta) + math.sqrt(theta * theta + 1.0))
                    cosine = 1.0 / math.sqrt(tangent * tangent + 1.0)
                    sine = tangent * cosine
                    for other_id in range(count):
                        left_val = work[other_id][first_id]
                        right_val = work[other_id][second_id]
                        work[other_id][first_id] = cosine * left_val - sine * right_val
                        work[other_id][second_id] = sine * left_val + cosine * right_val
                    for other_id in range(count):
                        left_val = work[first_id][other_id]
                        right_val = work[second_id][other_id]
                        work[first_id][other_id] = cosine * left_val - sine * right_val
                        work[second_id][other_id] = sine * left_val + cosine * right_val
                    for other_id in range(count):
                        left_val = vectors[other_id][first_id]
                        right_val = vectors[other_id][second_id]
                        vectors[other_id][first_id] = cosine * left_val - sine * right_val
                        vectors[other_id][second_id] = sine * left_val + cosine * right_val
    return ([work[idx_val][idx_val] for idx_val in range(count)], vectors)


def element_tables(point_count):
    poly_order = point_count - 1
    points = [-math.cos(math.pi * idx_val / poly_order) for idx_val in range(point_count)]
    for newton_id in range(100):
        updated = []
        for point in points:
            before, current = legendre_pair(poly_order, point)
            updated.append(point - (point * current - before) / (point_count * current))
        points = updated
    values = [legendre_pair(poly_order, point)[1] for point in points]
    weights = [2.0 / (poly_order * point_count * value**2) for value in values]
    derivative = [[0.0] * point_count for row_id in range(point_count)]
    for left_index in range(point_count):
        for right_index in range(point_count):
            if left_index != right_index:
                derivative[left_index][right_index] = values[left_index] / (
                    values[right_index] * (points[left_index] - points[right_index])
                )
    derivative[0][0] = -poly_order * point_count / 4.0
    derivative[poly_order][poly_order] = poly_order * point_count / 4.0
    stiffness = [
        [
            sum(
                (
                    derivative[inner_id][row_id] * weights[inner_id] * derivative[inner_id][col_id]
                    for inner_id in range(point_count)
                )
            )
            for col_id in range(point_count)
        ]
        for row_id in range(point_count)
    ]
    size_three = 3 * poly_order + 1
    stiff_three = [[0.0] * size_three for row_id in range(size_three)]
    mass_three = [0.0] * size_three
    for element in range(3):
        first_node = element * poly_order
        for row_id in range(point_count):
            mass_three[first_node + row_id] += weights[row_id]
            for col_id in range(point_count):
                stiff_three[first_node + row_id][first_node + col_id] += stiffness[row_id][col_id]
    keep = list(range(poly_order - 1, 2 * poly_order + 2))
    scale_half = [1.0 / math.sqrt(mass_three[idx_val]) for idx_val in keep]
    scaled = [
        [
            scale_half[row_id] * stiff_three[keep[row_id]][keep[col_id]] * scale_half[col_id]
            for col_id in range(len(keep))
        ]
        for row_id in range(len(keep))
    ]
    eigen_values, vectors = jacobi_eigen(scaled)
    transform = [
        [scale_half[row_id] * vectors[row_id][col_id] for col_id in range(len(keep))]
        for row_id in range(len(keep))
    ]
    return (weights, stiffness, eigen_values, transform)


def device_tables():
    tables = element_tables(NP)
    return tuple((jnp.asarray(table, dtype=jnp.float32) for table in tables))


def tensor_apply(matrix, tensor, node_axis):
    patterns = ("ai,ijkxyz->ajkxyz", "aj,ijkxyz->iakxyz", "ak,ijkxyz->ijaxyz")
    return jnp.einsum(patterns[node_axis], matrix, tensor, precision=HIGHEST)


def cut_out(tensor, begin_at, end_at, node_axis):
    return lax.slice_in_dim(tensor, begin_at, end_at, axis=node_axis)


def shift_in(local_part, remote_part, elem_axis, forward):
    elem_count = local_part.shape[elem_axis]
    if forward:
        return jnp.concatenate(
            [remote_part, cut_out(local_part, 0, elem_count - 1, elem_axis)], axis=elem_axis
        )
    return jnp.concatenate(
        [cut_out(local_part, 1, elem_count, elem_axis), remote_part], axis=elem_axis
    )


def boundary_pair(first_part, last_part, elem_axis):
    elem_count = last_part.shape[elem_axis]
    return jnp.concatenate(
        [
            cut_out(first_part, 0, 1, elem_axis),
            cut_out(last_part, elem_count - 1, elem_count, elem_axis),
        ],
        axis=elem_axis,
    )


def end_faces(vector, node_axis):
    return (cut_out(vector, 0, 1, node_axis), cut_out(vector, NP - 1, NP, node_axis))


def join_faces(vector, node_axis, elem_axis, low_face, high_face, from_left, from_right):
    new_low = low_face + shift_in(high_face, from_left, elem_axis, True)
    new_high = high_face + shift_in(low_face, from_right, elem_axis, False)
    return jnp.concatenate(
        [new_low, cut_out(vector, 1, NP - 1, node_axis), new_high], axis=node_axis
    )


def finish_assembly(vector, from_left, from_right):
    low_face, high_face = end_faces(vector, 0)
    vector = join_faces(vector, 0, 3, low_face, high_face, from_left, from_right)
    low_face, high_face = end_faces(vector, 1)
    padded = extended_2(boundary_pair(low_face, high_face, 4), (("grp", 4),), 1, False)
    vector = join_faces(
        vector, 1, 4, low_face, high_face, cut_out(padded, 0, 1, 4), cut_out(padded, 3, 4, 4)
    )
    low_face, high_face = end_faces(vector, 2)
    elem_count = vector.shape[5]
    return join_faces(
        vector,
        2,
        5,
        low_face,
        high_face,
        cut_out(high_face, elem_count - 1, elem_count, 5),
        cut_out(low_face, 0, 1, 5),
    )


def assemble(vector):
    low_face, high_face = end_faces(vector, 0)
    padded = extended_2(boundary_pair(low_face, high_face, 3), (("dev", 3),), 1, True)
    return finish_assembly(vector, cut_out(padded, 0, 1, 3), cut_out(padded, 3, 4, 3))


def mass_cube(weights):
    cube = weights[:, None, None] * weights[None, :, None] * weights[None, None, :]
    return cube[:, :, :, None, None, None]


def local_operator(vector, coefficient, weights, stiffness):
    weight_x = weights.reshape(NP, 1, 1, 1, 1, 1)
    weight_y = weights.reshape(1, NP, 1, 1, 1, 1)
    weight_z = weights.reshape(1, 1, NP, 1, 1, 1)
    stiff_term = tensor_apply(stiffness, vector, 0) * weight_y * weight_z
    stiff_term = stiff_term + tensor_apply(stiffness, vector, 1) * weight_x * weight_z
    stiff_term = stiff_term + tensor_apply(stiffness, vector, 2) * weight_x * weight_y
    return (
        coefficient[None, None, None] * stiff_term
        + MASS_SHIFT * weight_x * weight_y * weight_z * vector
    )


def widen(vector, node_axis, elem_axis, from_left, from_right):
    inner_low = cut_out(vector, 1, 2, node_axis)
    inner_high = cut_out(vector, NP - 2, NP - 1, node_axis)
    return jnp.concatenate(
        [
            shift_in(inner_high, from_left, elem_axis, True),
            vector,
            shift_in(inner_low, from_right, elem_axis, False),
        ],
        axis=node_axis,
    )


def extend(vector):
    padded = extended_2(
        boundary_pair(cut_out(vector, 1, 2, 0), cut_out(vector, NP - 2, NP - 1, 0), 3),
        (("dev", 3),),
        1,
        True,
    )
    vector = widen(vector, 0, 3, cut_out(padded, 0, 1, 3), cut_out(padded, 3, 4, 3))
    padded = extended_2(
        boundary_pair(cut_out(vector, 1, 2, 1), cut_out(vector, NP - 2, NP - 1, 1), 4),
        (("grp", 4),),
        1,
        False,
    )
    vector = widen(vector, 1, 4, cut_out(padded, 0, 1, 4), cut_out(padded, 3, 4, 4))
    elem_count = vector.shape[5]
    from_left = cut_out(cut_out(vector, NP - 2, NP - 1, 2), elem_count - 1, elem_count, 5)
    from_right = cut_out(cut_out(vector, 1, 2, 2), 0, 1, 5)
    return widen(vector, 2, 5, from_left, from_right)


def local_solve(extended, coefficient, eigen_values, transform):
    tensor = tensor_apply(transform.T, extended, 0)
    tensor = tensor_apply(transform.T, tensor, 1)
    tensor = tensor_apply(transform.T, tensor, 2)
    eigen_sum = (
        eigen_values[:, None, None] + eigen_values[None, :, None] + eigen_values[None, None, :]
    )
    tensor = tensor / (
        coefficient[None, None, None] * eigen_sum[:, :, :, None, None, None] + MASS_SHIFT
    )
    tensor = tensor_apply(transform, tensor, 0)
    tensor = tensor_apply(transform, tensor, 1)
    return tensor_apply(transform, tensor, 2)


def outer_layers(solved, node_axis):
    return (cut_out(solved, 0, 1, node_axis), cut_out(solved, NP + 1, NP + 2, node_axis))


def narrow(solved, node_axis, elem_axis, first_layer, last_layer, from_left, from_right):
    middle = cut_out(solved, 1, NP + 1, node_axis)
    add_one = shift_in(last_layer, from_left, elem_axis, True)
    add_six = shift_in(first_layer, from_right, elem_axis, False)
    return jnp.concatenate(
        [
            cut_out(middle, 0, 1, node_axis),
            cut_out(middle, 1, 2, node_axis) + add_one,
            cut_out(middle, 2, NP - 2, node_axis),
            cut_out(middle, NP - 2, NP - 1, node_axis) + add_six,
            cut_out(middle, NP - 1, NP, node_axis),
        ],
        axis=node_axis,
    )


def fold_inner(solved):
    first_layer, last_layer = outer_layers(solved, 2)
    elem_count = solved.shape[5]
    solved = narrow(
        solved,
        2,
        5,
        first_layer,
        last_layer,
        cut_out(last_layer, elem_count - 1, elem_count, 5),
        cut_out(first_layer, 0, 1, 5),
    )
    first_layer, last_layer = outer_layers(solved, 1)
    padded = extended_2(boundary_pair(first_layer, last_layer, 4), (("grp", 4),), 1, False)
    return narrow(
        solved, 1, 4, first_layer, last_layer, cut_out(padded, 0, 1, 4), cut_out(padded, 3, 4, 4)
    )


def coarse_solve(coarse_res, coarse_rows):
    shard_piece = jax.tree.map(
        lambda part: lax.all_gather(part, "dev", axis=0, tiled=True), coarse_res
    )
    block = lax.slice_in_dim(coarse_rows, 0, shard_piece.shape[0], axis=1)
    return jnp.zeros(coarse_rows.shape[0], jnp.float32) + jnp.dot(
        block, shard_piece, precision=HIGHEST
    )


def precondition(residual, coefficient, coarse_rows, tables):
    weights, stiffness, eigen_values, transform = tables
    solved = fold_inner(local_solve(extend(residual), coefficient, eigen_values, transform))
    cube = mass_cube(weights)
    element_sums = jnp.sum(cube * residual, axis=(0, 1, 2))
    coarse_count = coarse_rows.shape[0]
    elem_count = residual.shape[5]
    coarse_res = (
        jnp.sum(element_sums, axis=(0, 1))
        .reshape(coarse_count, elem_count // coarse_count)
        .sum(axis=1)
    )
    coarse_sol = coarse_solve(coarse_res, coarse_rows)
    spread = jnp.broadcast_to(
        coarse_sol[:, None], (coarse_count, elem_count // coarse_count)
    ).reshape(1, 1, elem_count)
    coarse_term = cube * spread[None, None, None]
    first_layer, last_layer = outer_layers(solved, 0)
    padded = extended_2(boundary_pair(first_layer, last_layer, 3), (("dev", 3),), 1, True)
    folded = narrow(
        solved, 0, 3, first_layer, last_layer, cut_out(padded, 0, 1, 3), cut_out(padded, 3, 4, 3)
    )
    return assemble(folded + coarse_term)


def inverse_multiplicity(first_row, total_rows, rows_here):
    layer_ids = jnp.arange(NP)
    shared = (layer_ids == 0) | (layer_ids == NP - 1)
    plain_mult = jnp.where(shared, 2.0, 1.0).astype(jnp.float32)
    row_ids = first_row + jnp.arange(rows_here)
    at_wall = (layer_ids[:, None] == 0) & (row_ids[None, :] == 0) | (
        layer_ids[:, None] == NP - 1
    ) & (row_ids[None, :] == total_rows - 1)
    row_mult = jnp.where(shared[:, None] & jnp.logical_not(at_wall), 2.0, 1.0).astype(jnp.float32)
    multiplicity = (
        plain_mult.reshape(NP, 1, 1, 1, 1, 1)
        * row_mult.reshape(1, NP, 1, 1, rows_here, 1)
        * plain_mult.reshape(1, 1, NP, 1, 1, 1)
    )
    return 1.0 / multiplicity


def local(forcing, coefficient, coarse_inverse):
    tables = device_tables()
    weights, stiffness = (tables[0], tables[1])
    rows_here = forcing.shape[4]
    inverse_mult = inverse_multiplicity(
        lax.axis_index("grp") * rows_here, lax.axis_size("grp") * rows_here, rows_here
    )

    def local_dot(left_vec, right_vec):
        return jnp.sum(left_vec * right_vec * inverse_mult)

    def rz_product(residual_now, precond_now):
        return lax.psum(local_dot(residual_now, precond_now), ("grp", "dev"))

    load = assemble(forcing)
    solution = jnp.zeros_like(load)
    residual = load
    precond = precondition(residual, coefficient, coarse_inverse, tables)
    direction = precond
    gamma_now = rz_product(residual, precond)
    for iteration in range(ITERS):
        image = assemble(local_operator(direction, coefficient, weights, stiffness))
        step_len = gamma_now / lax.psum(local_dot(direction, image), ("grp", "dev"))
        solution = solution + step_len * direction
        residual = residual - step_len * image
        if iteration + 1 < ITERS:
            precond = precondition(residual, coefficient, coarse_inverse, tables)
            gamma_next = rz_product(residual, precond)
            direction = precond + gamma_next / gamma_now * direction
            gamma_now = gamma_next
    return (solution, residual)


def solution(mesh):
    in_specs = (
        P(None, None, None, "dev", "grp", None),
        P("dev", "grp", None),
        P(("grp", "dev"), None),
    )
    out_specs = (P(None, None, None, "dev", "grp", None), P(None, None, None, "dev", "grp", None))
    return jax.shard_map(local, mesh=mesh, in_specs=in_specs, out_specs=out_specs, check_vma=False)
```

profile of v0, /device:TPU:1, one launch (start us, length us, event | category | flops | bytes accessed | tf_op | source)
XLA Modules:
  0.0 682.1 jit_solution(15650220745486282959)
XLA Ops:
  1.5 4.8 collective-permute-start
  6.3 10.2 %collective-permute-done = f32[1,8,8,1,1,128]{5,1,0,4,3,2:T(8,128)S(1)} collective-permute-done((f32[1,8,8,1,1,128]{5,1,0,4,3,2:T(8,128)S(1)}, f32[1,8,8,1,1,128]{5,1,0,4,3,2:T(8,128)S(1)}, u32[]{:S(2)}, u32[]{:S(2)}) %collective-permute-start) | collective-permute-done | bytes 32800 | tf_op jit(solution)/shard_map/ppermute | solution.py:23
  21.4 5.8 collective-permute-start.2
  30.2 3.8 collective-permute-done.3
  36.5 7.0 %collective-permute-start.5 = (f32[1,8,8,1,1,128]{5,1,0,4,3,2:T(8,128)S(1)}, f32[1,8,8,1,1,128]{5,1,0,4,3,2:T(8,128)S(1)}, u32[]{:S(2)}, u32[]{:S(2)}) collective-permute-start(f32[1,8,8,1,1,128]{5,1,0,4,3,2:T(8,128)S(1)} %get-tuple-element.102), channel_id=1, source_target_pairs={{1,0},{2,1},{3,2},{4,3},{5,4},{6,5},{7,6},{8,7},{9,8},{10,9},{11,1... | collective-permute-start | bytes 98312 | tf_op jit(solution)/shard_map/ppermute | solution.py:24
  51.8 61.1 %all-reduce = f32[1024]{0:T(1024)S(1)} all-reduce(f32[1024]{0:T(1024)S(1)} %dynamic-update-slice), channel_id=1, replica_groups=mesh['grp'=16,'dev'=32] {'dev'}, use_global_device_ids=true, to_apply=%add | all-reduce | flops 1024 | bytes 8192
  122.3 17.9 %collective-permute-start.8 = (f32[10,1,8,1,1,128]{5,2,1,0,4,3:T(8,128)S(1)}, f32[10,1,8,1,1,128]{5,2,1,0,4,3:T(8,128)S(1)}, u32[]{:S(2)}, u32[]{:S(2)}) collective-permute-start(f32[10,1,8,1,1,128]{5,2,1,0,4,3:T(8,128)S(1)} %get-tuple-element.41), channel_id=1, source_target_pairs={{0,32},{32,64},{64,96},{96,128},{128,160},{160,192},{192,224},{224... | collective-permute-start | bytes 122888 | tf_op jit(solution)/shard_map/ppermute | solution.py:23
  148.1 6.7 collective-permute-start.11
  157.9 7.0 %collective-permute-start.13 = (f32[1,8,8,1,1,128]{5,2,1,0,4,3:T(8,128)S(1)}, f32[1,8,8,1,1,128]{5,2,1,0,4,3:T(8,128)S(1)}, u32[]{:S(2)}, u32[]{:S(2)}) collective-permute-start(f32[1,8,8,1,1,128]{5,2,1,0,4,3:T(8,128)S(1)} %get-tuple-element.98), channel_id=1, source_target_pairs={{1,0},{2,1},{3,2},{4,3},{5,4},{6,5},{7,6},{8,7},{9,8},{10,9},{11,1... | collective-permute-start | bytes 98312 | tf_op jit(solution)/shard_map/ppermute | solution.py:24
  165.9 4.2 collective-permute-start.14
  173.2 3.7 collective-permute-done.15
  182.1 7.3 %collective-permute-start.17 = (f32[1,8,8,1,1,128]{5,1,0,4,3,2:T(8,128)S(1)}, f32[1,8,8,1,1,128]{5,1,0,4,3,2:T(8,128)S(1)}, u32[]{:S(2)}, u32[]{:S(2)}) collective-permute-start(f32[1,8,8,1,1,128]{5,1,0,4,3,2:T(8,128)S(1)} %get-tuple-element.88), channel_id=1, source_target_pairs={{1,0},{2,1},{3,2},{4,3},{5,4},{6,5},{7,6},{8,7},{9,8},{10,9},{11,1... | collective-permute-start | bytes 98312 | tf_op jit(solution)/shard_map/ppermute | solution.py:24
  196.3 3.8 collective-permute-done.19
  201.2 105.4 %all-reduce.2 = (f32[]{:T(128)}, f32[]{:T(128)}) all-reduce(f32[]{:T(128)} %get-tuple-element.7, f32[]{:T(128)} %get-tuple-element.6), channel_id=1, replica_groups=mesh['grp'=16,'dev'=32] {'grp','dev'}, use_global_device_ids=true, to_apply=%region_3.4 | all-reduce | flops 2 | bytes 16 | tf_op jit(solution)/shard_map/psum | solution.py:379
  310.0 6.7 collective-permute-start.21
  340.6 61.2 %all-reduce.1 = f32[1024]{0:T(1024)S(1)} all-reduce(f32[1024]{0:T(1024)S(1)} %dynamic-update-slice.1), channel_id=1, replica_groups=mesh['grp'=16,'dev'=32] {'dev'}, use_global_device_ids=true, to_apply=%add.1 | all-reduce | flops 1024 | bytes 8192
  404.7 6.7 collective-permute-start.27
  414.5 7.0 %collective-permute-start.29 = (f32[1,8,8,1,1,128]{5,1,0,4,3,2:T(8,128)S(1)}, f32[1,8,8,1,1,128]{5,1,0,4,3,2:T(8,128)S(1)}, u32[]{:S(2)}, u32[]{:S(2)}) collective-permute-start(f32[1,8,8,1,1,128]{5,1,0,4,3,2:T(8,128)S(1)} %get-tuple-element.76), channel_id=1, source_target_pairs={{1,0},{2,1},{3,2},{4,3},{5,4},{6,5},{7,6},{8,7},{9,8},{10,9},{11,1... | collective-permute-start | bytes 98312 | tf_op jit(solution)/shard_map/ppermute | solution.py:24
  422.5 19.6 %collective-permute-start.30 = (f32[8,1,8,1,1,128]{5,1,0,4,3,2:T(1,128)S(1)}, f32[8,1,8,1,1,128]{5,1,0,4,3,2:T(1,128)S(1)}, u32[]{:S(2)}, u32[]{:S(2)}) collective-permute-start(f32[8,1,8,1,1,128]{5,1,0,4,3,2:T(1,128)S(1)} %pad_maximum_fusion.19), channel_id=1, source_target_pairs={{0,32},{32,64},{64,96},{96,128},{128,160},{160,192},{192,224},{224... | collective-permute-start | bytes 98312 | tf_op jit(solution)/shard_map/ppermute | solution.py:23
  445.2 3.9 collective-permute-done.31
  450.2 102.5 %psum.30 = f32[]{:T(128)} all-reduce(f32[]{:T(128)} %multiply_reduce_fusion.1), channel_id=1, replica_groups=mesh['grp'=16,'dev'=32] {'grp','dev'}, use_global_device_ids=true, to_apply=%region_9.10 | all-reduce | flops 1 | bytes 8 | tf_op jit(solution)/shard_map/psum | solution.py:379
  558.0 6.7 collective-permute-start.33
  572.4 3.9 collective-permute-done.35
  577.4 101.3 %psum.31 = f32[]{:T(128)} all-reduce(f32[]{:T(128)} %multiply_reduce_fusion), channel_id=1, replica_groups=mesh['grp'=16,'dev'=32] {'grp','dev'}, use_global_device_ids=true, to_apply=%region_11.12 | all-reduce | flops 1 | bytes 8 | tf_op jit(solution)/shard_map/psum | solution.py:389
  (226 shorter events, 107.8 us)
Async XLA Ops:
  1.5 15.0 %collective-permute-start = (f32[1,8,8,1,1,128]{5,1,0,4,3,2:T(8,128)S(1)}, f32[1,8,8,1,1,128]{5,1,0,4,3,2:T(8,128)S(1)}, u32[]{:S(2)}, u32[]{:S(2)}) collective-permute-start(f32[1,8,8,1,1,128]{5,1,0,4,3,2:T(8,128)S(1)} %copy.124), channel_id=1, source_target_pairs={{0,1},{1,2},{2,3},{3,4},{4,5},{5,6},{6,7},{7,8},{8,9},{9,10},{10,1... | collective-permute-start | bytes 98312 | tf_op jit(solution)/shard_map/ppermute | solution.py:23
  21.4 6.8 collective-permute-start.2
  34.6 9.0 %collective-permute-start.4 = (f32[1,8,8,1,1,128]{5,1,0,4,3,2:T(8,128)S(1)}, f32[1,8,8,1,1,128]{5,1,0,4,3,2:T(8,128)S(1)}, u32[]{:S(2)}, u32[]{:S(2)}) collective-permute-start(f32[1,8,8,1,1,128]{5,1,0,4,3,2:T(8,128)S(1)} %get-tuple-element.101), channel_id=1, source_target_pairs={{0,1},{1,2},{2,3},{3,4},{4,5},{5,6},{6,7},{7,8},{8,9},{9,10},{10,1... | collective-permute-start | bytes 98312 | tf_op jit(solution)/shard_map/ppermute | solution.py:23
  36.5 8.0 %collective-permute-start.5 = (f32[1,8,8,1,1,128]{5,1,0,4,3,2:T(8,128)S(1)}, f32[1,8,8,1,1,128]{5,1,0,4,3,2:T(8,128)S(1)}, u32[]{:S(2)}, u32[]{:S(2)}) collective-permute-start(f32[1,8,8,1,1,128]{5,1,0,4,3,2:T(8,128)S(1)} %get-tuple-element.102), channel_id=1, source_target_pairs={{1,0},{2,1},{3,2},{4,3},{5,4},{6,5},{7,6},{8,7},{9,8},{10,9},{11,1... | collective-permute-start | bytes 98312 | tf_op jit(solution)/shard_map/ppermute | solution.py:24
  44.6 68.3 %collective-permute-start.6 = (f32[10,1,8,1,1,128]{5,1,0,4,3,2:T(1,128)S(1)}, f32[10,1,8,1,1,128]{5,1,0,4,3,2:T(1,128)S(1)}, u32[]{:S(2)}, u32[]{:S(2)}) collective-permute-start(f32[10,1,8,1,1,128]{5,1,0,4,3,2:T(1,128)S(1)} %get-tuple-element.51), channel_id=1, source_target_pairs={{0,32},{32,64},{64,96},{96,128},{128,160},{160,192},{192,224},{224... | collective-permute-start | bytes 122888 | tf_op jit(solution)/shard_map/ppermute | solution.py:23
  47.3 65.5 %collective-permute-start.7 = (f32[10,1,8,1,1,128]{5,1,0,4,3,2:T(1,128)S(1)}, f32[10,1,8,1,1,128]{5,1,0,4,3,2:T(1,128)S(1)}, u32[]{:S(2)}, u32[]{:S(2)}) collective-permute-start(f32[10,1,8,1,1,128]{5,1,0,4,3,2:T(1,128)S(1)} %get-tuple-element.52), channel_id=1, source_target_pairs={{32,0},{64,32},{96,64},{128,96},{160,128},{192,160},{224,192},{256... | collective-permute-start | bytes 122888 | tf_op jit(solution)/shard_map/ppermute | solution.py:24
  122.3 20.2 %collective-permute-start.8 = (f32[10,1,8,1,1,128]{5,2,1,0,4,3:T(8,128)S(1)}, f32[10,1,8,1,1,128]{5,2,1,0,4,3:T(8,128)S(1)}, u32[]{:S(2)}, u32[]{:S(2)}) collective-permute-start(f32[10,1,8,1,1,128]{5,2,1,0,4,3:T(8,128)S(1)} %get-tuple-element.41), channel_id=1, source_target_pairs={{0,32},{32,64},{64,96},{96,128},{128,160},{160,192},{192,224},{224... | collective-permute-start | bytes 122888 | tf_op jit(solution)/shard_map/ppermute | solution.py:23
  146.0 8.8 %collective-permute-start.10 = (f32[1,8,8,1,1,128]{5,2,1,0,4,3:T(8,128)S(1)}, f32[1,8,8,1,1,128]{5,2,1,0,4,3:T(8,128)S(1)}, u32[]{:S(2)}, u32[]{:S(2)}) collective-permute-start(f32[1,8,8,1,1,128]{5,2,1,0,4,3:T(8,128)S(1)} %get-tuple-element.49), channel_id=1, source_target_pairs={{0,1},{1,2},{2,3},{3,4},{4,5},{5,6},{6,7},{7,8},{8,9},{9,10},{10,1... | collective-permute-start | bytes 98312 | tf_op jit(solution)/shard_map/ppermute | solution.py:23
  148.1 7.7 %collective-permute-start.11 = (f32[1,8,8,1,1,128]{5,2,1,0,4,3:T(8,128)S(1)}, f32[1,8,8,1,1,128]{5,2,1,0,4,3:T(8,128)S(1)}, u32[]{:S(2)}, u32[]{:S(2)}) collective-permute-start(f32[1,8,8,1,1,128]{5,2,1,0,4,3:T(8,128)S(1)} %get-tuple-element.48), channel_id=1, source_target_pairs={{1,0},{2,1},{3,2},{4,3},{5,4},{6,5},{7,6},{8,7},{9,8},{10,9},{11,1... | collective-permute-start | bytes 98312 | tf_op jit(solution)/shard_map/ppermute | solution.py:24
  156.0 8.9 %collective-permute-start.12 = (f32[1,8,8,1,1,128]{5,2,1,0,4,3:T(8,128)S(1)}, f32[1,8,8,1,1,128]{5,2,1,0,4,3:T(8,128)S(1)}, u32[]{:S(2)}, u32[]{:S(2)}) collective-permute-start(f32[1,8,8,1,1,128]{5,2,1,0,4,3:T(8,128)S(1)} %get-tuple-element.97), channel_id=1, source_target_pairs={{0,1},{1,2},{2,3},{3,4},{4,5},{5,6},{6,7},{7,8},{8,9},{9,10},{10,1... | collective-permute-start | bytes 98312 | tf_op jit(solution)/shard_map/ppermute | solution.py:23
  157.9 8.0 %collective-permute-start.13 = (f32[1,8,8,1,1,128]{5,2,1,0,4,3:T(8,128)S(1)}, f32[1,8,8,1,1,128]{5,2,1,0,4,3:T(8,128)S(1)}, u32[]{:S(2)}, u32[]{:S(2)}) collective-permute-start(f32[1,8,8,1,1,128]{5,2,1,0,4,3:T(8,128)S(1)} %get-tuple-element.98), channel_id=1, source_target_pairs={{1,0},{2,1},{3,2},{4,3},{5,4},{6,5},{7,6},{8,7},{9,8},{10,9},{11,1... | collective-permute-start | bytes 98312 | tf_op jit(solution)/shard_map/ppermute | solution.py:24
  180.2 9.2 %collective-permute-start.16 = (f32[1,8,8,1,1,128]{5,1,0,4,3,2:T(8,128)S(1)}, f32[1,8,8,1,1,128]{5,1,0,4,3,2:T(8,128)S(1)}, u32[]{:S(2)}, u32[]{:S(2)}) collective-permute-start(f32[1,8,8,1,1,128]{5,1,0,4,3,2:T(8,128)S(1)} %get-tuple-element.87), channel_id=1, source_target_pairs={{0,1},{1,2},{2,3},{3,4},{4,5},{5,6},{6,7},{7,8},{8,9},{9,10},{10,1... | collective-permute-start | bytes 98312 | tf_op jit(solution)/shard_map/ppermute | solution.py:23
  182.1 8.3 %collective-permute-start.17 = (f32[1,8,8,1,1,128]{5,1,0,4,3,2:T(8,128)S(1)}, f32[1,8,8,1,1,128]{5,1,0,4,3,2:T(8,128)S(1)}, u32[]{:S(2)}, u32[]{:S(2)}) collective-permute-start(f32[1,8,8,1,1,128]{5,1,0,4,3,2:T(8,128)S(1)} %get-tuple-element.88), channel_id=1, source_target_pairs={{1,0},{2,1},{3,2},{4,3},{5,4},{6,5},{7,6},{8,7},{9,8},{10,9},{11,1... | collective-permute-start | bytes 98312 | tf_op jit(solution)/shard_map/ppermute | solution.py:24
  308.0 8.6 %collective-permute-start.20 = (f32[1,8,8,1,1,128]{5,1,0,4,3,2:T(8,128)S(1)}, f32[1,8,8,1,1,128]{5,1,0,4,3,2:T(8,128)S(1)}, u32[]{:S(2)}, u32[]{:S(2)}) collective-permute-start(f32[1,8,8,1,1,128]{5,1,0,4,3,2:T(8,128)S(1)} %get-tuple-element.77), channel_id=1, source_target_pairs={{0,1},{1,2},{2,3},{3,4},{4,5},{5,6},{6,7},{7,8},{8,9},{9,10},{10,1... | collective-permute-start | bytes 98312 | tf_op jit(solution)/shard_map/ppermute | solution.py:23
  310.0 7.7 %collective-permute-start.21 = (f32[1,8,8,1,1,128]{5,1,0,4,3,2:T(8,128)S(1)}, f32[1,8,8,1,1,128]{5,1,0,4,3,2:T(8,128)S(1)}, u32[]{:S(2)}, u32[]{:S(2)}) collective-permute-start(f32[1,8,8,1,1,128]{5,1,0,4,3,2:T(8,128)S(1)} %get-tuple-element.78), channel_id=1, source_target_pairs={{1,0},{2,1},{3,2},{4,3},{5,4},{6,5},{7,6},{8,7},{9,8},{10,9},{11,1... | collective-permute-start | bytes 98312 | tf_op jit(solution)/shard_map/ppermute | solution.py:24
  334.5 67.4 %collective-permute-start.25 = (f32[10,1,8,1,1,128]{5,1,0,4,3,2:T(1,128)S(1)}, f32[10,1,8,1,1,128]{5,1,0,4,3,2:T(1,128)S(1)}, u32[]{:S(2)}, u32[]{:S(2)}) collective-permute-start(f32[10,1,8,1,1,128]{5,1,0,4,3,2:T(1,128)S(1)} %get-tuple-element.35), channel_id=1, source_target_pairs={{32,0},{64,32},{96,64},{128,96},{160,128},{192,160},{224,192},{256... | collective-permute-start | bytes 122888 | tf_op jit(solution)/shard_map/ppermute | solution.py:24
  336.4 65.4 %collective-permute-start.24 = (f32[10,1,8,1,1,128]{5,1,0,4,3,2:T(1,128)S(1)}, f32[10,1,8,1,1,128]{5,1,0,4,3,2:T(1,128)S(1)}, u32[]{:S(2)}, u32[]{:S(2)}) collective-permute-start(f32[10,1,8,1,1,128]{5,1,0,4,3,2:T(1,128)S(1)} %get-tuple-element.36), channel_id=1, source_target_pairs={{0,32},{32,64},{64,96},{96,128},{128,160},{160,192},{192,224},{224... | collective-permute-start | bytes 122888 | tf_op jit(solution)/shard_map/ppermute | solution.py:23
  402.4 9.0 %collective-permute-start.26 = (f32[1,8,8,1,1,128]{5,1,0,4,3,2:T(8,128)S(1)}, f32[1,8,8,1,1,128]{5,1,0,4,3,2:T(8,128)S(1)}, u32[]{:S(2)}, u32[]{:S(2)}) collective-permute-start(f32[1,8,8,1,1,128]{5,1,0,4,3,2:T(8,128)S(1)} %get-tuple-element.44), channel_id=1, source_target_pairs={{0,1},{1,2},{2,3},{3,4},{4,5},{5,6},{6,7},{7,8},{8,9},{9,10},{10,1... | collective-permute-start | bytes 98312 | tf_op jit(solution)/shard_map/ppermute | solution.py:23
  404.7 7.7 %collective-permute-start.27 = (f32[1,8,8,1,1,128]{5,1,0,4,3,2:T(8,128)S(1)}, f32[1,8,8,1,1,128]{5,1,0,4,3,2:T(8,128)S(1)}, u32[]{:S(2)}, u32[]{:S(2)}) collective-permute-start(f32[1,8,8,1,1,128]{5,1,0,4,3,2:T(8,128)S(1)} %get-tuple-element.43), channel_id=1, source_target_pairs={{1,0},{2,1},{3,2},{4,3},{5,4},{6,5},{7,6},{8,7},{9,8},{10,9},{11,1... | collective-permute-start | bytes 98312 | tf_op jit(solution)/shard_map/ppermute | solution.py:24
  412.6 8.9 %collective-permute-start.28 = (f32[1,8,8,1,1,128]{5,1,0,4,3,2:T(8,128)S(1)}, f32[1,8,8,1,1,128]{5,1,0,4,3,2:T(8,128)S(1)}, u32[]{:S(2)}, u32[]{:S(2)}) collective-permute-start(f32[1,8,8,1,1,128]{5,1,0,4,3,2:T(8,128)S(1)} %get-tuple-element.75), channel_id=1, source_target_pairs={{0,1},{1,2},{2,3},{3,4},{4,5},{5,6},{6,7},{7,8},{8,9},{9,10},{10,1... | collective-permute-start | bytes 98312 | tf_op jit(solution)/shard_map/ppermute | solution.py:23
  414.5 8.0 %collective-permute-start.29 = (f32[1,8,8,1,1,128]{5,1,0,4,3,2:T(8,128)S(1)}, f32[1,8,8,1,1,128]{5,1,0,4,3,2:T(8,128)S(1)}, u32[]{:S(2)}, u32[]{:S(2)}) collective-permute-start(f32[1,8,8,1,1,128]{5,1,0,4,3,2:T(8,128)S(1)} %get-tuple-element.76), channel_id=1, source_target_pairs={{1,0},{2,1},{3,2},{4,3},{5,4},{6,5},{7,6},{8,7},{9,8},{10,9},{11,1... | collective-permute-start | bytes 98312 | tf_op jit(solution)/shard_map/ppermute | solution.py:24
  422.5 20.6 %collective-permute-start.30 = (f32[8,1,8,1,1,128]{5,1,0,4,3,2:T(1,128)S(1)}, f32[8,1,8,1,1,128]{5,1,0,4,3,2:T(1,128)S(1)}, u32[]{:S(2)}, u32[]{:S(2)}) collective-permute-start(f32[8,1,8,1,1,128]{5,1,0,4,3,2:T(1,128)S(1)} %pad_maximum_fusion.19), channel_id=1, source_target_pairs={{0,32},{32,64},{64,96},{96,128},{128,160},{160,192},{192,224},{224... | collective-permute-start | bytes 98312 | tf_op jit(solution)/shard_map/ppermute | solution.py:23
  556.1 8.6 %collective-permute-start.32 = (f32[1,8,8,1,1,128]{5,1,0,4,3,2:T(8,128)S(1)}, f32[1,8,8,1,1,128]{5,1,0,4,3,2:T(8,128)S(1)}, u32[]{:S(2)}, u32[]{:S(2)}) collective-permute-start(f32[1,8,8,1,1,128]{5,1,0,4,3,2:T(8,128)S(1)} %get-tuple-element.61), channel_id=1, source_target_pairs={{0,1},{1,2},{2,3},{3,4},{4,5},{5,6},{6,7},{7,8},{8,9},{9,10},{10,1... | collective-permute-start | bytes 98312 | tf_op jit(solution)/shard_map/ppermute | solution.py:23
  558.0 7.7 %collective-permute-start.33 = (f32[1,8,8,1,1,128]{5,1,0,4,3,2:T(8,128)S(1)}, f32[1,8,8,1,1,128]{5,1,0,4,3,2:T(8,128)S(1)}, u32[]{:S(2)}, u32[]{:S(2)}) collective-permute-start(f32[1,8,8,1,1,128]{5,1,0,4,3,2:T(8,128)S(1)} %get-tuple-element.62), channel_id=1, source_target_pairs={{1,0},{2,1},{3,2},{4,3},{5,4},{6,5},{7,6},{8,7},{9,8},{10,9},{11,1... | collective-permute-start | bytes 98312 | tf_op jit(solution)/shard_map/ppermute | solution.py:24
  (21 other events, 230.6 us)
where the time goes:
time: 684 us; the launch traced here: 682 us
  blocking collectives  431 us (63%)
  starting transfers between devices  160 us (23%)
  waiting for transfers between devices  49.8 us (7%)
  matrix products  15.8 us (2%)
  local copies, waits for them, and re-layouts  10 us (1%)
  other arithmetic  8.7 us (1%)
    psum x2, blocking collectives, rz_product(): return lax.psum(local_dot(residual_now, precond_now), ('grp', 'dev'))  208 us
    unnamed x2, blocking collectives  122 us
    psum x1, blocking collectives, local(): step_len = gamma_now / lax.psum(local_dot(direction, image), ('grp', 'dev'))  101 us
    ppermute x18, starting transfers between devices, extended_2(): before = lax.ppermute(last, axis, up)  84.1 us
    ppermute x18, starting transfers between devices, extended_2(): after = lax.ppermute(leading, axis, down)  75.8 us
    ppermute x18, waiting for transfers between devices, extended_2(): after = lax.ppermute(leading, axis, down)  34.7 us
    dot_general x18, matrix products, tensor_apply(): return jnp.einsum(patterns[node_axis], matrix, tensor, precision=HIGHEST)  15.4 us
    ppermute x18, waiting for transfers between devices, extended_2(): before = lax.ppermute(last, axis, up)  15 us
  transfers between devices with their start and end apart: 36, of which 22 were waited for; matrix products, arithmetic and copies ran while one was open for 1% of the time, Pallas kernels for 0%

commit v1 on v0

v1 whole, which is shorter than its diff:
```python
import functools
import math

import jax
import jax.numpy as jnp
import ml_dtypes
import numpy as np
from jax import lax
from jax.experimental import pallas as pl
from jax.experimental.pallas import tpu as pltpu
from jax.sharding import PartitionSpec as P

NP = 8
NX = NP + 2
LANES = 128
MASS_SHIFT = 0.1
HIGHEST = lax.Precision.HIGHEST


def legendre_pair(order, point):
    before = 1.0
    current = point
    for degree in range(2, order + 1):
        before, current = (
            current,
            ((2 * degree - 1) * point * current - (degree - 1) * before) / degree,
        )
    return (before, current)


def jacobi_eigen(matrix_in):
    count = len(matrix_in)
    work = [list(row_vals) for row_vals in matrix_in]
    vectors = [
        [1.0 if row_id == col_id else 0.0 for col_id in range(count)] for row_id in range(count)
    ]
    for sweep_id in range(14):
        for first_id in range(count - 1):
            for second_id in range(first_id + 1, count):
                off_value = work[first_id][second_id]
                if abs(off_value) > 1e-300:
                    theta = (work[second_id][second_id] - work[first_id][first_id]) / (
                        2.0 * off_value
                    )
                    sign_val = 1.0 if theta >= 0.0 else -1.0
                    tangent = sign_val / (abs(theta) + math.sqrt(theta * theta + 1.0))
                    cosine = 1.0 / math.sqrt(tangent * tangent + 1.0)
                    sine = tangent * cosine
                    for other_id in range(count):
                        left_val = work[other_id][first_id]
                        right_val = work[other_id][second_id]
                        work[other_id][first_id] = cosine * left_val - sine * right_val
                        work[other_id][second_id] = sine * left_val + cosine * right_val
                    for other_id in range(count):
                        left_val = work[first_id][other_id]
                        right_val = work[second_id][other_id]
                        work[first_id][other_id] = cosine * left_val - sine * right_val
                        work[second_id][other_id] = sine * left_val + cosine * right_val
                    for other_id in range(count):
                        left_val = vectors[other_id][first_id]
                        right_val = vectors[other_id][second_id]
                        vectors[other_id][first_id] = cosine * left_val - sine * right_val
                        vectors[other_id][second_id] = sine * left_val + cosine * right_val
    return ([work[idx_val][idx_val] for idx_val in range(count)], vectors)


def element_tables(point_count):
    poly_order = point_count - 1
    points = [-math.cos(math.pi * idx_val / poly_order) for idx_val in range(point_count)]
    for newton_id in range(100):
        updated = []
        for point in points:
            before, current = legendre_pair(poly_order, point)
            updated.append(point - (point * current - before) / (point_count * current))
        points = updated
    values = [legendre_pair(poly_order, point)[1] for point in points]
    weights = [2.0 / (poly_order * point_count * value**2) for value in values]
    derivative = [[0.0] * point_count for row_id in range(point_count)]
    for left_index in range(point_count):
        for right_index in range(point_count):
            if left_index != right_index:
                derivative[left_index][right_index] = values[left_index] / (
                    values[right_index] * (points[left_index] - points[right_index])
                )
    derivative[0][0] = -poly_order * point_count / 4.0
    derivative[poly_order][poly_order] = poly_order * point_count / 4.0
    stiffness = [
        [
            sum(
                (
                    derivative[inner_id][row_id] * weights[inner_id] * derivative[inner_id][col_id]
                    for inner_id in range(point_count)
                )
            )
            for col_id in range(point_count)
        ]
        for row_id in range(point_count)
    ]
    size_three = 3 * poly_order + 1
    stiff_three = [[0.0] * size_three for row_id in range(size_three)]
    mass_three = [0.0] * size_three
    for element in range(3):
        first_node = element * poly_order
        for row_id in range(point_count):
            mass_three[first_node + row_id] += weights[row_id]
            for col_id in range(point_count):
                stiff_three[first_node + row_id][first_node + col_id] += stiffness[row_id][col_id]
    keep = list(range(poly_order - 1, 2 * poly_order + 2))
    scale_half = [1.0 / math.sqrt(mass_three[idx_val]) for idx_val in keep]
    scaled = [
        [
            scale_half[row_id] * stiff_three[keep[row_id]][keep[col_id]] * scale_half[col_id]
            for col_id in range(len(keep))
        ]
        for row_id in range(len(keep))
    ]
    eigen_values, vectors = jacobi_eigen(scaled)
    transform = [
        [scale_half[row_id] * vectors[row_id][col_id] for col_id in range(len(keep))]
        for row_id in range(len(keep))
    ]
    return (weights, stiffness, eigen_values, transform)


KROWS = 112
PAIRS = ((0, 1), (8, 9), (2, 3), (4, 5), (6, 7))
SIDES = ((1, 0), (-1, 0), (0, 1), (0, -1), (1, 1), (1, -1), (-1, 1), (-1, -1))


def split_bf16(matrix):
    high = matrix.astype(ml_dtypes.bfloat16)
    low = (matrix - high.astype(np.float64)).astype(ml_dtypes.bfloat16)
    return high, low


def stacked(matrix):
    high, low = split_bf16(matrix)
    return np.concatenate(
        [np.concatenate([high, high], 1), np.concatenate([low, np.zeros_like(low)], 1)], 0
    )


@functools.lru_cache(maxsize=None)
def constants():
    weights, stiffness, eigen_values, transform = (
        np.array(table, dtype=np.float64) for table in element_tables(NP)
    )
    forward = np.zeros((KROWS, KROWS))
    lam_rows = np.zeros((KROWS,))
    for b in range(NX):
        for c in range(NX):
            row = b * NX + c
            lam_rows[row] = eigen_values[b] + eigen_values[c]
            for j in range(NX):
                for k in range(NX):
                    if k == 0:
                        col = 80 + j
                    elif k == NX - 1:
                        col = 96 + j
                    else:
                        col = j * NP + k - 1
                    forward[row, col] = transform[j, b] * transform[k, c]
    diag_w = np.diag(weights)
    plane = np.kron(stiffness, diag_w) + np.kron(diag_w, stiffness)
    table = np.zeros((128, LANES), np.float32)
    table[:KROWS] = lam_rows[:, None]
    table[KROWS : KROWS + NP] = weights[:, None]
    half = np.ones((NP,))
    half[0] = half[-1] = 0.5
    table[KROWS + NP :] = half[:, None]
    return dict(
        weights=[float(v) for v in weights],
        stiffness=stiffness,
        eigen=[float(v) for v in eigen_values],
        transform=transform,
        forward=stacked(forward),
        back=stacked(forward.T),
        plane=stacked(plane),
        table=table,
    )


def combine(scalars, vectors):
    total = None
    for scalar, vector in zip(scalars, vectors):
        term = float(scalar) * vector
        total = term if total is None else total + term
    return total


def dot_split(matrix, value):
    rows = value.shape[0]
    high = value.astype(jnp.bfloat16)
    low = (value - high.astype(jnp.float32)).astype(jnp.bfloat16)
    out = jnp.dot(
        matrix, jnp.concatenate([high, low], axis=0), preferred_element_type=jnp.float32
    )
    return out[:rows] + out[rows:]


def lane_fold(value):
    value = value + pltpu.roll(value, 64, 1)
    return value + pltpu.roll(value, 32, 1)


def next_lane(value, axis):
    return pltpu.roll(value, LANES - 1, axis)


def previous_lane(value, axis):
    return pltpu.roll(value, 1, axis)


def face_range(step, low, middle, high):
    return {1: high, -1: low, 0: middle}[step]


EQ_X = (slice(0, 2), slice(0, 8), slice(6, 8))
EQ_Y = (slice(0, 16), slice(0, 64), slice(48, 64))
QF_X = (slice(0, 2), slice(1, 9), slice(8, 10))
QF_Y = (slice(0, 16), slice(8, 72), slice(64, 80))
Q_X = (slice(0, 1), slice(0, 8), slice(7, 8))
Q_Y = (slice(0, 8), slice(0, 64), slice(56, 64))


def kernel(
    n_grp,
    n_dev,
    f_ref,
    coef_ref,
    rows_ref,
    table_ref,
    fwd_ref,
    back_ref,
    plane_ref,
    sol_ref,
    res_ref,
    u0,
    u1,
    u2,
    e0,
    e1,
    s0,
    s1,
    z0,
    z1,
    work,
    inv_ref,
    x1,
    y1,
    c1,
    x2,
    y2,
    c2,
    x3,
    y3,
    c3,
    x4,
    y4,
    c4,
    x5,
    y5,
    c5,
    coarse_a,
    coarse_b,
    dots_a,
    dots_b,
    dots_c,
    dots_d,
    send_sem,
    recv_sem,
    bulk_send,
    bulk_recv,
):
    tabs = constants()
    weights = tabs["weights"]
    stiff = tabs["stiffness"]
    trans = tabs["transform"]
    eigen = tabs["eigen"]
    grp = lax.axis_index("grp")
    dev = lax.axis_index("dev")

    def dev_at(step):
        return lax.rem(dev + step + n_dev, n_dev)

    def grp_at(step):
        return lax.rem(grp + step + n_grp, n_grp)

    barrier = pltpu.get_barrier_semaphore()

    def greet_dev(step, carry):
        pl.semaphore_signal(
            barrier, inc=1, device_id=(grp, lax.rem(dev + step, n_dev)),
            device_id_type=pl.DeviceIdType.MESH,
        )
        return carry

    def greet_grp(step, carry):
        pl.semaphore_signal(
            barrier, inc=1, device_id=(lax.rem(grp + step, n_grp), dev),
            device_id_type=pl.DeviceIdType.MESH,
        )
        return carry

    lax.fori_loop(1, n_dev, greet_dev, 0)
    lax.fori_loop(1, n_grp, greet_grp, 0)
    for dx, dy in SIDES[4:]:
        pl.semaphore_signal(
            barrier, inc=1, device_id=(grp_at(dy), dev_at(dx)),
            device_id_type=pl.DeviceIdType.MESH,
        )

    def exchange(number, source, x_ranges, y_ranges, x_buf, y_buf, c_buf):
        copies = []
        for index, (dx, dy) in enumerate(SIDES):
            src = source.at[
                face_range(dx, *x_ranges), face_range(dy, *y_ranges), :
            ]
            if dy == 0:
                dst = x_buf.at[0 if dx == 1 else 1]
            elif dx == 0:
                dst = y_buf.at[0 if dy == 1 else 1]
            else:
                dst = c_buf.at[0 if dx == 1 else 1, 0 if dy == 1 else 1]
            copy = pltpu.make_async_remote_copy(
                src_ref=src,
                dst_ref=dst,
                send_sem=send_sem.at[number, index],
                recv_sem=recv_sem.at[number, index],
                device_id=(grp_at(dy), dev_at(dx)),
                device_id_type=pl.DeviceIdType.MESH,
            )
            copy.start()
            copies.append(copy)
        return copies

    def arrive(copies):
        for copy in copies:
            copy.wait_recv()

    def spread_row(buf, number, along_dev):
        count = n_dev if along_dev else n_grp
        me = dev if along_dev else grp

        def body(step, carry):
            other = lax.rem(me + step, count)
            pltpu.make_async_remote_copy(
                src_ref=buf.at[me],
                dst_ref=buf.at[me],
                send_sem=bulk_send.at[number],
                recv_sem=bulk_recv.at[number],
                device_id=(grp, other) if along_dev else (other, dev),
                device_id_type=pl.DeviceIdType.MESH,
            ).start()
            return carry

        lax.fori_loop(1, count, body, 0)

    def bulk_wait(buf, sem, count):
        part = buf.at[pl.ds(0, count - 1)]
        pltpu.make_async_copy(part, part, sem).wait()

    low_wall = jnp.where(grp == 0, 0.0, 1.0).astype(jnp.float32)
    high_wall = jnp.where(grp == n_grp - 1, 0.0, 1.0).astype(jnp.float32)
    coef = coef_ref[...]
    w_k = table_ref[KROWS : KROWS + NP, :]
    half_k = table_ref[KROWS + NP :, :]
    lane = lax.broadcasted_iota(jnp.int32, (1, LANES), 1)

    def assemble_z(ref):
        top = ref[:, pl.ds(0, NP, stride=NP), :]
        bottom = ref[:, pl.ds(NP - 1, NP, stride=NP), :]
        ref[:, pl.ds(0, NP, stride=NP), :] = top + previous_lane(bottom, 2)
        ref[:, pl.ds(NP - 1, NP, stride=NP), :] = bottom + next_lane(top, 2)

    u0[...] = f_ref[...]
    assemble_z(u0)
    pl.semaphore_wait(barrier, n_dev - 1 + n_grp - 1 + 4)
    round_1 = exchange(0, u0, EQ_X, EQ_Y, x1, y1, c1)

    lam_rows = table_ref[0:KROWS, :]
    for a in range(NX):
        inv_ref[a] = 1.0 / (coef * (lam_rows + eigen[a]) + MASS_SHIFT)
    zero_rows = jnp.zeros((128 - 80, LANES), jnp.float32)
    for i in range(NX):
        e0[i, 80:128, :] = zero_rows
        e1[i, 80:128, :] = zero_rows
        s0[i, 80:128, :] = zero_rows
        s1[i, 80:128, :] = zero_rows

    def extend_into(ext, own, x_buf, y_buf, c_buf):
        for i in range(NX):
            if i == 0:
                row = x_buf[0, 0]
                low = c_buf[0, 0, 0]
                high = c_buf[0, 1, 0]
            elif i == NX - 1:
                row = x_buf[1, 1]
                low = c_buf[1, 0, 1]
                high = c_buf[1, 1, 1]
            else:
                row = own[i - 1]
                low = y_buf[0, i - 1]
                high = y_buf[1, i - 1]
                if i == 1:
                    row = row + x_buf[0, 1]
                    low = low + c_buf[0, 0, 1]
                    high = high + c_buf[0, 1, 1]
                elif i == NX - 2:
                    row = row + x_buf[1, 0]
                    low = low + c_buf[1, 0, 0]
                    high = high + c_buf[1, 1, 0]
            low = low * low_wall
            high = high * high_wall
            ext[i, 0:8, :] = low[0:8]
            ext[i, 8:16, :] = row[0:8] + low[8:16]
            ext[i, 16:64, :] = row[8:56]
            ext[i, 64:72, :] = row[56:64] + high[0:8]
            ext[i, 72:80, :] = high[8:16]

    def start_coarse(ext, buf, number):
        total = None
        for i in range(NP):
            line = combine(
                weights, [ext[i + 1, 8 + NP * j : 16 + NP * j, :] for j in range(NP)]
            )
            total = weights[i] * line if total is None else total + weights[i] * line
        total = total * w_k
        elem = lax.broadcasted_iota(jnp.int32, (LANES, LANES), 0)
        place = lax.broadcasted_iota(jnp.int32, (LANES, LANES), 1)
        group = jnp.where(
            place == lax.rem(dev, 4) * 32 + lax.shift_right_logical(elem, 2), 1.0, 0.0
        ).astype(jnp.float32)
        sums = jnp.dot(total, group, precision=HIGHEST, preferred_element_type=jnp.float32)
        buf[dev] = jnp.sum(sums, axis=0, keepdims=True)
        spread_row(buf, number, True)

    def finish_coarse(buf, number):
        bulk_wait(buf, bulk_recv.at[number], n_dev)
        total = None
        for block in range(n_dev // 4):
            first = 4 * block
            row = (buf[first] + buf[first + 1]) + (buf[first + 2] + buf[first + 3])
            term = rows_ref[:, block * LANES : (block + 1) * LANES] * row
            total = term if total is None else total + term
        sums = jnp.sum(total, axis=1, keepdims=True)
        unknown = lax.broadcasted_iota(jnp.int32, (32, LANES), 0)
        elem = lax.broadcasted_iota(jnp.int32, (32, LANES), 1)
        mine = lax.shift_right_logical(elem, 2) == unknown
        sol = jnp.sum(jnp.where(mine, sums, 0.0), axis=0, keepdims=True)
        node = lax.broadcasted_iota(jnp.int32, (NP, LANES), 0)
        beside = jnp.where(node == 0, previous_lane(sol, 1), 0.0) + jnp.where(
            node == NP - 1, next_lane(sol, 1), 0.0
        )
        return w_k * (sol + beside)

    even = [a for a in range(NX) if abs(trans[0, a] - trans[9, a]) < abs(trans[0, a] + trans[9, a])]
    odd = [a for a in range(NX) if a not in even]

    def local_solve(ext, out):
        for pair in PAIRS:
            parts = []
            for i in pair:
                front = previous_lane(ext[i, pl.ds(6, 16, stride=NP), :], 1)
                behind = next_lane(ext[i, pl.ds(1, 16, stride=NP), :], 1)
                parts.append(jnp.concatenate([ext[i, 0:80, :], front, behind], axis=0))
            got = dot_split(fwd_ref[...], jnp.concatenate(parts, axis=1))
            work[pair[0]] = got[:, 0:LANES]
            work[pair[1]] = got[:, LANES:]

        def middle(block, carry):
            rows = pl.ds(pl.multiple_of(block * 8, 8), 8)
            vals = [work[i, rows, :] for i in range(NX)]
            plus = [vals[i] + vals[NX - 1 - i] for i in range(5)]
            minus = [vals[i] - vals[NX - 1 - i] for i in range(5)]
            modes = {}
            for a in range(NX):
                source = plus if a in even else minus
                modes[a] = combine(trans[:5, a], source) * inv_ref[a, rows, :]
            for i in range(5):
                sym = combine(trans[i, even], [modes[a] for a in even])
                anti = combine(trans[i, odd], [modes[a] for a in odd])
                work[i, rows, :] = sym + anti
                work[NX - 1 - i, rows, :] = sym - anti
            return carry

        lax.fori_loop(0, KROWS // 8, middle, 0)
        for pair in PAIRS:
            got = dot_split(
                back_ref[...], jnp.concatenate([work[pair[0]], work[pair[1]]], axis=1)
            )
            for side, i in enumerate(pair):
                part = got[:, side * LANES : (side + 1) * LANES]
                out[i, 0:80, :] = part[0:80]
                at_6 = pl.ds(6, 16, stride=NP)
                at_1 = pl.ds(1, 16, stride=NP)
                at_0 = pl.ds(0, 16, stride=NP)
                at_7 = pl.ds(7, 16, stride=NP)
                out[i, at_6, :] = out[i, at_6, :] + next_lane(part[80:96], 1)
                out[i, at_1, :] = out[i, at_1, :] + previous_lane(part[96:112], 1)
                top = out[i, at_0, :]
                bottom = out[i, at_7, :]
                out[i, at_0, :] = top + previous_lane(bottom, 1)
                out[i, at_7, :] = bottom + next_lane(top, 1)

    def add_coarse(out, coarse):
        for i in range(NP):
            for j in range(NP):
                rows = slice(8 + NP * j, 16 + NP * j)
                out[i + 1, rows, :] = out[i + 1, rows, :] + (weights[i] * weights[j]) * coarse

    def fold_field(out, i, x_buf, y_buf, c_buf):
        row = out[i + 1, 8:72, :]
        low = y_buf[0, i]
        high = y_buf[1, i]
        if i < 2:
            row = row + x_buf[0, i]
            low = low + c_buf[0, 0, i]
            high = high + c_buf[0, 1, i]
        elif i >= 6:
            row = row + x_buf[1, i - 6]
            low = low + c_buf[1, 0, i - 6]
            high = high + c_buf[1, 1, i - 6]
        return jnp.concatenate(
            [row[0:16] + low * low_wall, row[16:48], row[48:64] + high * high_wall], axis=0
        )

    def operate(field, out):
        total = jnp.zeros((NP, LANES), jnp.float32)
        for pair in ((0, 7), (1, 6), (2, 5), (3, 4)):
            got = dot_split(
                plane_ref[...], jnp.concatenate([field[pair[0]], field[pair[1]]], axis=1)
            )
            out[pair[0]] = got[:, 0:LANES]
            out[pair[1]] = got[:, LANES:]
        for j in range(NP):
            rows = slice(NP * j, NP * j + NP)
            vals = [field[i, rows, :] for i in range(NP)]
            plus = [vals[i] + vals[NP - 1 - i] for i in range(4)]
            minus = [vals[i] - vals[NP - 1 - i] for i in range(4)]
            w_yz = weights[j] * w_k
            coef_yz = coef * w_yz
            for i in range(4):
                sym = combine([(stiff[i, m] + stiff[i, 7 - m]) / 2 for m in range(4)], plus)
                anti = combine([(stiff[i, m] - stiff[i, 7 - m]) / 2 for m in range(4)], minus)
                for at, value in ((i, sym + anti), (7 - i, sym - anti)):
                    result = (
                        value * coef_yz
                        + (weights[at] * coef) * out[at, rows, :]
                        + (MASS_SHIFT * weights[at]) * (w_yz * vals[at])
                    )
                    out[at, rows, :] = result
                    total = total + result * vals[at]
        return total

    def inverse_mult(i, j):
        scale = 0.5 if i in (0, NP - 1) else 1.0
        if j == 0:
            return scale * (1.0 - 0.5 * low_wall)
        if j == NP - 1:
            return scale * (1.0 - 0.5 * high_wall)
        return scale

    def product(left, right):
        total = jnp.zeros((NP, LANES), jnp.float32)
        for j in range(NP):
            line = None
            for i in range(NP):
                term = left(i, j) * right(i, j)
                if i in (0, NP - 1):
                    term = 0.5 * term
                line = term if line is None else line + term
            if j == 0:
                line = line * (1.0 - 0.5 * low_wall)
            elif j == NP - 1:
                line = line * (1.0 - 0.5 * high_wall)
            total = total + line
        return total * half_k

    def from_ext(ext):
        return lambda i, j: ext[i + 1, 8 + NP * j : 16 + NP * j, :]

    def from_field(field):
        return lambda i, j: field[i, NP * j : NP * j + NP, :]

    def pack_dots(totals):
        packed = None
        for index, total in enumerate(totals):
            row = lane_fold(jnp.sum(total, axis=0, keepdims=True))
            mine = (lane >= 32 * index) & (lane < 32 * index + 32)
            row = jnp.where(mine, row, 0.0)
            packed = row if packed is None else packed + row
        return packed

    def unpack_dot(row, index):
        mine = (lane >= 32 * index) & (lane < 32 * index + 32)
        return jnp.sum(jnp.where(mine, row, 0.0), axis=1, keepdims=True)

    def add_slots(buf, count):
        rows = [buf[index] for index in range(count)]
        while len(rows) > 1:
            rows = [rows[index] + rows[index + 1] for index in range(0, len(rows), 2)]
        return rows[0]

    arrive(round_1)
    extend_into(e0, u0, x1, y1, c1)
    start_coarse(e0, coarse_a, 0)
    local_solve(e0, s0)
    add_coarse(s0, finish_coarse(coarse_a, 0))
    round_2 = exchange(1, s0, QF_X, QF_Y, x2, y2, c2)
    arrive(round_2)
    for i in range(NP):
        z0[i] = fold_field(s0, i, x2, y2, c2)

    delta_part = operate(z0, u1)
    assemble_z(u1)
    round_3 = exchange(2, u1, EQ_X, EQ_Y, x3, y3, c3)
    gamma_part = product(from_ext(e0), from_field(z0))
    dots_a[dev] = pack_dots([gamma_part, delta_part])
    spread_row(dots_a, 2, True)
    arrive(round_3)
    extend_into(e1, u1, x3, y3, c3)

    start_coarse(e1, coarse_b, 1)
    local_solve(e1, s1)
    add_coarse(s1, finish_coarse(coarse_b, 1))
    round_4 = exchange(3, s1, QF_X, QF_Y, x4, y4, c4)
    bulk_wait(dots_a, bulk_recv.at[2], n_dev)
    dots_b[grp] = add_slots(dots_a, n_dev)
    spread_row(dots_b, 3, False)
    bulk_wait(dots_b, bulk_recv.at[3], n_grp)
    first_dots = add_slots(dots_b, n_grp)
    gamma_0 = unpack_dot(first_dots, 0)
    delta_0 = unpack_dot(first_dots, 1)
    alpha_0 = gamma_0 / delta_0
    arrive(round_4)
    for i in range(NP):
        z1[i] = z0[i] - alpha_0 * fold_field(s1, i, x4, y4, c4)

    zeta_part = operate(z1, u2)
    assemble_z(u2)
    round_5 = exchange(4, u2, Q_X, Q_Y, x5, y5, c5)
    for i in range(NP):
        res_ref[i] = e0[i + 1, 8:72, :] - alpha_0 * e1[i + 1, 8:72, :]
    gamma_part = product(from_field(res_ref), from_field(z1))
    eta_part = product(from_ext(e1), from_field(z1))
    dots_c[dev] = pack_dots([gamma_part, eta_part, zeta_part])
    spread_row(dots_c, 4, True)
    bulk_wait(dots_c, bulk_recv.at[4], n_dev)
    dots_d[grp] = add_slots(dots_c, n_dev)
    spread_row(dots_d, 5, False)
    arrive(round_5)
    for i in range(NP):
        row = u2[i]
        low = y5[0, i]
        high = y5[1, i]
        if i == 0:
            row = row + x5[0, 0]
            low = low + c5[0, 0, 0]
            high = high + c5[0, 1, 0]
        elif i == NP - 1:
            row = row + x5[1, 0]
            low = low + c5[1, 0, 0]
            high = high + c5[1, 1, 0]
        e0[i, 0:8, :] = row[0:8] + low * low_wall
        e0[i, 8:56, :] = row[8:56]
        e0[i, 56:64, :] = row[56:64] + high * high_wall
    bulk_wait(dots_d, bulk_recv.at[5], n_grp)
    last_dots = add_slots(dots_d, n_grp)
    gamma_1 = unpack_dot(last_dots, 0)
    eta = unpack_dot(last_dots, 1)
    zeta = unpack_dot(last_dots, 2)
    beta = gamma_1 / gamma_0
    alpha_1 = gamma_1 / (zeta + beta * (2.0 * eta + beta * delta_0))
    scale_0 = alpha_0 + alpha_1 * beta
    for i in range(NP):
        sol_ref[i] = scale_0 * z0[i] + alpha_1 * z1[i]
        res_ref[i] = res_ref[i] - alpha_1 * (e0[i, 0:64, :] + beta * e1[i + 1, 8:72, :])

    for copies in (round_1, round_2, round_3, round_4, round_5):
        for copy in copies:
            copy.wait_send()
    for number, (buf, count) in enumerate(
        (
            (coarse_a, n_dev),
            (coarse_b, n_dev),
            (dots_a, n_dev),
            (dots_b, n_grp),
            (dots_c, n_dev),
            (dots_d, n_grp),
        )
    ):
        bulk_wait(buf, bulk_send.at[number], count)


def local(n_grp, n_dev, forcing, coefficient, coarse_inverse):
    tabs = constants()
    field = (NP, NP * NP, LANES)
    vmem = pl.BlockSpec(memory_space=pltpu.VMEM)

    def buffers(depth):
        return [
            pltpu.VMEM((2, depth, NP * NP, LANES), jnp.float32),
            pltpu.VMEM((2, NP, NP * depth, LANES), jnp.float32),
            pltpu.VMEM((2, 2, depth, NP * depth, LANES), jnp.float32),
        ]

    ext = pltpu.VMEM((NX, 128, LANES), jnp.float32)
    full = pltpu.VMEM(field, jnp.float32)
    modes = pltpu.VMEM((NX, KROWS, LANES), jnp.float32)
    along_dev = pltpu.VMEM((n_dev, 1, LANES), jnp.float32)
    along_grp = pltpu.VMEM((n_grp, 1, LANES), jnp.float32)
    out = jax.ShapeDtypeStruct(field, jnp.float32)
    columns = n_dev * coarse_inverse.shape[0]
    solved, residual = pl.pallas_call(
        functools.partial(kernel, n_grp, n_dev),
        out_shape=(out, out),
        in_specs=[vmem] * 7,
        out_specs=(vmem, vmem),
        scratch_shapes=[
            full, full, full, ext, ext, ext, ext, full, full, modes, modes,
            *buffers(2), *buffers(2), *buffers(2), *buffers(2), *buffers(1),
            along_dev, along_dev, along_dev, along_grp, along_dev, along_grp,
            pltpu.SemaphoreType.DMA((5, 8)),
            pltpu.SemaphoreType.DMA((5, 8)),
            pltpu.SemaphoreType.DMA((6,)),
            pltpu.SemaphoreType.DMA((6,)),
        ],
        compiler_params=pltpu.CompilerParams(
            collective_id=0, has_side_effects=True, vmem_limit_bytes=40 * 1024 * 1024
        ),
    )(
        forcing.reshape(field),
        coefficient.reshape(1, LANES),
        coarse_inverse[:, :columns],
        jnp.asarray(tabs["table"]),
        jnp.asarray(tabs["forward"]),
        jnp.asarray(tabs["back"]),
        jnp.asarray(tabs["plane"]),
    )
    return solved.reshape(forcing.shape), residual.reshape(forcing.shape)


def solution(mesh):
    in_specs = (
        P(None, None, None, "dev", "grp", None),
        P("dev", "grp", None),
        P(("grp", "dev"), None),
    )
    out_specs = (P(None, None, None, "dev", "grp", None), P(None, None, None, "dev", "grp", None))
    return jax.shard_map(
        functools.partial(local, mesh.shape["grp"], mesh.shape["dev"]),
        mesh=mesh,
        in_specs=in_specs,
        out_specs=out_specs,
        check_vma=False,
    )
```

time: 684 us -> 70.1 us (0.10)
  blocking collectives: 431 us -> 0 us
  starting transfers between devices: 160 us -> 0 us
  Pallas kernels: 0 us -> 61.8 us
  waiting for transfers between devices: 49.8 us -> 0 us
  matrix products: 15.8 us -> 0 us
  other arithmetic: 8.7 us -> 0 us
    psum x3 -> x0, blocking collectives: 309 us -> none  [the longest x2 208 us: rz_product(): return lax.psum(local_dot(residual_now, precond_now), ('grp', 'dev'))]
    ppermute x36 -> x0, starting transfers between devices: 160 us -> none  [the longest x18 84.1 us: extended_2(): before = lax.ppermute(last, axis, up)]
    unnamed x2 -> x0, blocking collectives: 122 us -> none
    pallas_call x0 -> x1, Pallas kernels: none -> 61.8 us  [local(): pl.pallas_call(functools.partial(kernel, n_grp, n_dev), out_shape=(out, o...]
    ppermute x36 -> x0, waiting for transfers between devices: 49.8 us -> none  [the longest x18 34.7 us: extended_2(): after = lax.ppermute(leading, axis, down)]
    dot_general x20 -> x0, matrix products: 15.8 us -> none  [the longest x18 15.4 us: tensor_apply(): return jnp.einsum(patterns[node_axis], matrix, tensor, precision=HIGHEST)]
  transfers between devices with their start and end apart: 36 -> 0, of which waited for: 22 -> 0; matrix products, arithmetic and copies ran while one was open for 1% -> 0% of each run, Pallas kernels for 0% -> 0%
where the time goes in v1:
time: 70.1 us; the launch traced here: 69.8 us
  Pallas kernels  61.8 us (88%)
  local copies, waits for them, and re-layouts  7.3 us (10%)
    pallas_call x1, Pallas kernels, local(): pl.pallas_call(functools.partial(kernel, n_grp, n_dev), out_shape=(out, o...  61.8 us
    unnamed x16, local copies, waits for them, and re-layouts  7.3 us

profile of v1, /device:TPU:1, one launch (start us, length us, event | category | flops | bytes accessed | tf_op | source)
XLA Modules:
  0.0 69.8 jit_solution(18311821126892667662)
XLA Ops:
  0.6 0.0 copy-start.6
  0.6 0.6 copy-done.6
  1.3 0.0 copy-start
  1.3 0.9 %copy-done = f32[8,8,8,1,1,128]{5,4,3,2,1,0:T(1,128)S(1)} copy-done((f32[8,8,8,1,1,128]{5,4,3,2,1,0:T(1,128)S(1)}, f32[8,8,8,1,1,128]{5,4,3,2,1,0:T(1,128)}, u32[]{:S(2)}) %copy-start) | copy-done | bytes 262168
  2.2 0.0 copy-start.1
  2.2 0.9 %copy-done.1 = f32[32,1024]{1,0:T(8,128)S(1)} copy-done((f32[32,1024]{1,0:T(8,128)S(1)}, f32[32,1024]{1,0:T(8,128)}, u32[]{:S(2)}) %copy-start.1) | copy-done | bytes 131096
  3.1 0.0 copy-start.2
  3.1 0.9 %copy-done.2 = bf16[224,224]{1,0:T(8,128)(2,1)S(1)} copy-done((bf16[224,224]{1,0:T(8,128)(2,1)S(1)}, bf16[224,224]{1,0:T(8,128)(2,1)}, u32[]{:S(2)}) %copy-start.2) | copy-done | bytes 100376
  4.0 0.0 copy-start.3
  4.0 0.9 %copy-done.3 = bf16[224,224]{1,0:T(8,128)(2,1)S(1)} copy-done((bf16[224,224]{1,0:T(8,128)(2,1)S(1)}, bf16[224,224]{1,0:T(8,128)(2,1)}, u32[]{:S(2)}) %copy-start.3) | copy-done | bytes 100376
  4.9 0.0 copy-start.4
  4.9 0.8 %copy-done.4 = f32[128,128]{1,0:T(8,128)S(1)} copy-done((f32[128,128]{1,0:T(8,128)S(1)}, f32[128,128]{1,0:T(8,128)}, u32[]{:S(2)}) %copy-start.4) | copy-done | bytes 65560
  5.8 0.0 copy-start.5
  5.8 0.8 %copy-done.5 = bf16[128,128]{1,0:T(8,128)(2,1)S(1)} copy-done((bf16[128,128]{1,0:T(8,128)(2,1)S(1)}, bf16[128,128]{1,0:T(8,128)(2,1)}, u32[]{:S(2)}) %copy-start.5) | copy-done | bytes 32792
  6.5 61.8 %shard_map.86 = (f32[8,64,128]{2,1,0:T(8,128)S(1)}, f32[8,64,128]{2,1,0:T(8,128)S(1)}) custom-call(f32[8,64,128]{2,1,0:T(8,128)S(1)} %bitcast.8, f32[1,128]{1,0:T(1,128)S(1)} %bitcast.11, f32[32,1024]{1,0:T(8,128)S(1)} %copy-done.1, f32[128,128]{1,0:T(8,128)S(1)} %copy-done.4, bf16[224,224]{1,0:T(8,128)(2,1)S(1)} %copy-done.3, ...), custom_call_target="tpu_custom_call" | custom-call | tf_op jit(solution)/shard_map/pallas_call | solution.py:715
  68.4 0.7 %copy.13 = f32[8,8,8,1,1,128]{5,4,3,2,1,0:T(1,128)} copy(f32[8,8,8,1,1,128]{5,4,3,2,1,0:T(1,128)S(1)} %bitcast.10) | data formatting | bytes 524288
  69.1 0.7 %copy.14 = f32[8,8,8,1,1,128]{5,4,3,2,1,0:T(1,128)} copy(f32[8,8,8,1,1,128]{5,4,3,2,1,0:T(1,128)S(1)} %bitcast.9) | data formatting | bytes 524288
Async XLA Ops:
  0.6 0.7 copy-start.6
  1.3 0.9 %copy-start = (f32[8,8,8,1,1,128]{5,4,3,2,1,0:T(1,128)S(1)}, f32[8,8,8,1,1,128]{5,4,3,2,1,0:T(1,128)}, u32[]{:S(2)}) copy-start(f32[8,8,8,1,1,128]{5,4,3,2,1,0:T(1,128)} %param.7) | copy-start | bytes 786436
  2.2 0.9 %copy-start.1 = (f32[32,1024]{1,0:T(8,128)S(1)}, f32[32,1024]{1,0:T(8,128)}, u32[]{:S(2)}) copy-start(f32[32,1024]{1,0:T(8,128)} %rows_ref.1) | copy-start | bytes 393220
  3.1 0.9 %copy-start.2 = (bf16[224,224]{1,0:T(8,128)(2,1)S(1)}, bf16[224,224]{1,0:T(8,128)(2,1)}, u32[]{:S(2)}) copy-start(bf16[224,224]{1,0:T(8,128)(2,1)} %constant.10.clone.back_ref) | copy-start | bytes 301060
  4.0 0.9 %copy-start.3 = (bf16[224,224]{1,0:T(8,128)(2,1)S(1)}, bf16[224,224]{1,0:T(8,128)(2,1)}, u32[]{:S(2)}) copy-start(bf16[224,224]{1,0:T(8,128)(2,1)} %constant.9.clone.fwd_ref) | copy-start | bytes 301060
  4.9 0.8 %copy-start.4 = (f32[128,128]{1,0:T(8,128)S(1)}, f32[128,128]{1,0:T(8,128)}, u32[]{:S(2)}) copy-start(f32[128,128]{1,0:T(8,128)} %constant.8.clone.table_ref) | copy-start | bytes 196612
  5.8 0.8 %copy-start.5 = (bf16[128,128]{1,0:T(8,128)(2,1)S(1)}, bf16[128,128]{1,0:T(8,128)(2,1)}, u32[]{:S(2)}) copy-start(bf16[128,128]{1,0:T(8,128)(2,1)} %constant.11.clone.plane_ref) | copy-start | bytes 98308

commit v2 on v1

--- a/solution.py
+++ b/solution.py
@@ -123,8 +123,16 @@
 
 
 KROWS = 112
-PAIRS = ((0, 1), (8, 9), (2, 3), (4, 5), (6, 7))
-SIDES = ((1, 0), (-1, 0), (0, 1), (0, -1), (1, 1), (1, -1), (-1, 1), (-1, -1))
+OUTER = ((0, 1), (8, 9))
+INNER = ((2, 3), (4, 5), (6, 7))
+CORNERS = ((1, 1), (1, -1), (-1, 1), (-1, -1))
+ALONG_X = ((1, 0), (-1, 0))
+ALONG_Y = ((0, 1), (0, -1))
+SIDES = CORNERS + ALONG_X + ALONG_Y
+FORWARD = 128
+BACK = FORWARD + 2 * KROWS
+PLANE = BACK + 2 * KROWS
+TABLE_ROWS = PLANE + 2 * 64
 
 
 def split_bf16(matrix):
@@ -133,11 +141,12 @@
     return high, low
 
 
-def stacked(matrix):
-    high, low = split_bf16(matrix)
-    return np.concatenate(
-        [np.concatenate([high, high], 1), np.concatenate([low, np.zeros_like(low)], 1)], 0
-    )
+def padded_parts(matrix):
+    parts = np.zeros((2 * matrix.shape[0], LANES), np.float32)
+    for index, part in enumerate(split_bf16(matrix)):
+        rows = slice(index * matrix.shape[0], (index + 1) * matrix.shape[0])
+        parts[rows, : matrix.shape[1]] = part.astype(np.float32)
+    return parts
 
 
 @functools.lru_cache(maxsize=None)
@@ -173,10 +182,9 @@
         stiffness=stiffness,
         eigen=[float(v) for v in eigen_values],
         transform=transform,
-        forward=stacked(forward),
-        back=stacked(forward.T),
-        plane=stacked(plane),
-        table=table,
+        table=np.concatenate(
+            [table, padded_parts(forward), padded_parts(forward.T), padded_parts(plane)], 0
+        ),
     )
 
 
@@ -192,8 +200,13 @@
     rows = value.shape[0]
     high = value.astype(jnp.bfloat16)
     low = (value - high.astype(jnp.float32)).astype(jnp.bfloat16)
+    parts = [high, low]
+    gap = matrix.shape[1] // 2 - rows
+    if gap > 0:
+        zeros = jnp.zeros((gap, value.shape[1]), jnp.bfloat16)
+        parts = [high, zeros, low, zeros]
     out = jnp.dot(
-        matrix, jnp.concatenate([high, low], axis=0), preferred_element_type=jnp.float32
+        matrix, jnp.concatenate(parts, axis=0), preferred_element_type=jnp.float32
     )
     return out[:rows] + out[rows:]
 
@@ -226,15 +239,19 @@
 def kernel(
     n_grp,
     n_dev,
-    f_ref,
+    f_hbm,
+    coef_hbm,
+    rows_hbm,
+    table_hbm,
+    sol_ref,
+    res_ref,
     coef_ref,
     rows_ref,
     table_ref,
     fwd_ref,
     back_ref,
     plane_ref,
-    sol_ref,
-    res_ref,
+    pick_ref,
     u0,
     u1,
     u2,
@@ -261,12 +278,15 @@
     x5,
     y5,
     c5,
-    coarse_a,
-    coarse_b,
+    part_a,
+    part_b,
+    sums_a,
+    sums_b,
     dots_a,
     dots_b,
     dots_c,
     dots_d,
+    load_sem,
     send_sem,
     recv_sem,
     bulk_send,
@@ -286,6 +306,20 @@
     def grp_at(step):
         return lax.rem(grp + step + n_grp, n_grp)
 
+    loads = [
+        pltpu.make_async_copy(src, dst, load_sem.at[index])
+        for index, (src, dst) in enumerate(
+            (
+                (f_hbm, u0),
+                (table_hbm, table_ref),
+                (coef_hbm, coef_ref),
+                (rows_hbm, rows_ref),
+            )
+        )
+    ]
+    for load in loads:
+        load.start()
+
     barrier = pltpu.get_barrier_semaphore()
 
     def greet_dev(step, carry):
@@ -304,15 +338,16 @@
 
     lax.fori_loop(1, n_dev, greet_dev, 0)
     lax.fori_loop(1, n_grp, greet_grp, 0)
-    for dx, dy in SIDES[4:]:
+    for dx, dy in CORNERS:
         pl.semaphore_signal(
             barrier, inc=1, device_id=(grp_at(dy), dev_at(dx)),
             device_id_type=pl.DeviceIdType.MESH,
         )
 
-    def exchange(number, source, x_ranges, y_ranges, x_buf, y_buf, c_buf):
+    def exchange(number, sides, source, x_ranges, y_ranges, x_buf, y_buf, c_buf):
         copies = []
-        for index, (dx, dy) in enumerate(SIDES):
+        for dx, dy in sides:
+            index = SIDES.index((dx, dy))
             src = source.at[
                 face_range(dx, *x_ranges), face_range(dy, *y_ranges), :
             ]
@@ -338,33 +373,33 @@
         for copy in copies:
             copy.wait_recv()
 
+    def send_row(src, dst, number, where):
+        pltpu.make_async_remote_copy(
+            src_ref=src,
+            dst_ref=dst,
+            send_sem=bulk_send.at[number],
+            recv_sem=bulk_recv.at[number],
+            device_id=where,
+            device_id_type=pl.DeviceIdType.MESH,
+        ).start()
+
     def spread_row(buf, number, along_dev):
         count = n_dev if along_dev else n_grp
         me = dev if along_dev else grp
 
         def body(step, carry):
             other = lax.rem(me + step, count)
-            pltpu.make_async_remote_copy(
-                src_ref=buf.at[me],
-                dst_ref=buf.at[me],
-                send_sem=bulk_send.at[number],
-                recv_sem=bulk_recv.at[number],
-                device_id=(grp, other) if along_dev else (other, dev),
-                device_id_type=pl.DeviceIdType.MESH,
-            ).start()
+            send_row(buf.at[me], buf.at[me], number, (grp, other) if along_dev else (other, dev))
             return carry
 
         lax.fori_loop(1, count, body, 0)
 
     def bulk_wait(buf, sem, count):
-        part = buf.at[pl.ds(0, count - 1)]
+        part = buf.at[pl.ds(0, count)]
         pltpu.make_async_copy(part, part, sem).wait()
 
     low_wall = jnp.where(grp == 0, 0.0, 1.0).astype(jnp.float32)
     high_wall = jnp.where(grp == n_grp - 1, 0.0, 1.0).astype(jnp.float32)
-    coef = coef_ref[...]
-    w_k = table_ref[KROWS : KROWS + NP, :]
-    half_k = table_ref[KROWS + NP :, :]
     lane = lax.broadcasted_iota(jnp.int32, (1, LANES), 1)
 
     def assemble_z(ref):
@@ -373,11 +408,33 @@
         ref[:, pl.ds(0, NP, stride=NP), :] = top + previous_lane(bottom, 2)
         ref[:, pl.ds(NP - 1, NP, stride=NP), :] = bottom + next_lane(top, 2)
 
-    u0[...] = f_ref[...]
+    loads[0].wait()
     assemble_z(u0)
     pl.semaphore_wait(barrier, n_dev - 1 + n_grp - 1 + 4)
-    round_1 = exchange(0, u0, EQ_X, EQ_Y, x1, y1, c1)
-
+    round_1 = exchange(0, SIDES, u0, EQ_X, EQ_Y, x1, y1, c1)
+    for load in loads[1:]:
+        load.wait()
+
+    coef = coef_ref[...]
+    w_k = table_ref[KROWS : KROWS + NP, :]
+    half_k = table_ref[KROWS + NP : FORWARD, :]
+    for ref, first in ((fwd_ref, FORWARD), (back_ref, BACK)):
+        high = table_ref[first : first + KROWS, :].astype(jnp.bfloat16)
+        low = table_ref[first + KROWS : first + 2 * KROWS, :].astype(jnp.bfloat16)
+        ref[0:KROWS, 0:LANES] = high
+        ref[0:KROWS, LANES:] = high
+        ref[KROWS:, 0:LANES] = low
+        ref[KROWS:, LANES:] = jnp.zeros_like(low)
+    high = table_ref[PLANE : PLANE + 64, :]
+    plane_ref[0:64, :] = (high + pltpu.roll(high, 64, 1)).astype(jnp.bfloat16)
+    plane_ref[64:, :] = table_ref[PLANE + 64 : PLANE + 128, :].astype(jnp.bfloat16)
+    place = lax.broadcasted_iota(jnp.int32, (LANES, LANES), 0)
+    elem = lax.broadcasted_iota(jnp.int32, (LANES, LANES), 1)
+    for index in range(3):
+        block = lax.rem(dev + index + 3, 4)
+        pick_ref[:, index * LANES : (index + 1) * LANES] = jnp.where(
+            place == block * 32 + lax.shift_right_logical(elem, 2), 1.0, 0.0
+        ).astype(jnp.float32)
     lam_rows = table_ref[0:KROWS, :]
     for a in range(NX):
         inv_ref[a] = 1.0 / (coef * (lam_rows + eigen[a]) + MASS_SHIFT)
@@ -388,8 +445,8 @@
         s0[i, 80:128, :] = zero_rows
         s1[i, 80:128, :] = zero_rows
 
-    def extend_into(ext, own, x_buf, y_buf, c_buf):
-        for i in range(NX):
+    def extend_into(ext, layers, own, x_buf, y_buf, c_buf):
+        for i in layers:
             if i == 0:
                 row = x_buf[0, 0]
                 low = c_buf[0, 0, 0]
@@ -418,47 +475,87 @@
             ext[i, 64:72, :] = row[56:64] + high[0:8]
             ext[i, 72:80, :] = high[8:16]
 
-    def start_coarse(ext, buf, number):
+    def start_coarse(ext, part, sums, number):
         total = None
         for i in range(NP):
             line = combine(
                 weights, [ext[i + 1, 8 + NP * j : 16 + NP * j, :] for j in range(NP)]
             )
             total = weights[i] * line if total is None else total + weights[i] * line
-        total = total * w_k
-        elem = lax.broadcasted_iota(jnp.int32, (LANES, LANES), 0)
-        place = lax.broadcasted_iota(jnp.int32, (LANES, LANES), 1)
-        group = jnp.where(
-            place == lax.rem(dev, 4) * 32 + lax.shift_right_logical(elem, 2), 1.0, 0.0
-        ).astype(jnp.float32)
-        sums = jnp.dot(total, group, precision=HIGHEST, preferred_element_type=jnp.float32)
-        buf[dev] = jnp.sum(sums, axis=0, keepdims=True)
-        spread_row(buf, number, True)
-
-    def finish_coarse(buf, number):
-        bulk_wait(buf, bulk_recv.at[number], n_dev)
-        total = None
-        for block in range(n_dev // 4):
-            first = 4 * block
-            row = (buf[first] + buf[first + 1]) + (buf[first + 2] + buf[first + 3])
-            term = rows_ref[:, block * LANES : (block + 1) * LANES] * row
-            total = term if total is None else total + term
-        sums = jnp.sum(total, axis=1, keepdims=True)
+        total = jnp.sum(total * w_k, axis=0, keepdims=True)
         unknown = lax.broadcasted_iota(jnp.int32, (32, LANES), 0)
         elem = lax.broadcasted_iota(jnp.int32, (32, LANES), 1)
         mine = lax.shift_right_logical(elem, 2) == unknown
-        sol = jnp.sum(jnp.where(mine, sums, 0.0), axis=0, keepdims=True)
+        column = jnp.sum(jnp.where(mine, total, 0.0), axis=1, keepdims=True)
+        count = n_dev // 4
+        pieces = [
+            jnp.sum(rows_ref[:, m * LANES : (m + 1) * LANES] * column, axis=0, keepdims=True)
+            for m in range(count)
+        ]
+        for m in range(count):
+            first = jnp.where(lane >= 96, pieces[(m - 1) % count], pieces[m])
+            last = jnp.where(lane < 32, pieces[(m + 1) % count], pieces[m])
+            for index, row in enumerate((first, pieces[m], pieces[m], last)):
+                part[4 * m + index] = row
+        sums[1, dev] = part[dev]
+        up = grp_at(1)
+        down = grp_at(-1)
+
+        def send(step, carry):
+            other = lax.rem(dev + step, n_dev)
+            send_row(part.at[other], sums.at[0, dev], number, (up, other))
+            send_row(part.at[other], sums.at[2, dev], number + 2, (down, other))
+            return carry
+
+        def send_own(step, carry):
+            other = lax.rem(dev + step, n_dev)
+            send_row(part.at[other], sums.at[1, dev], number + 1, (grp, other))
+            return send(step, carry)
+
+        lax.fori_loop(1, n_dev, send_own, 0)
+        send(0, 0)
+
+    def coarse_wait(sums, sem, number):
+        bulk_wait(sums.at[0], sem.at[number], n_dev)
+        bulk_wait(sums.at[1], sem.at[number + 1], n_dev - 1)
+        bulk_wait(sums.at[2], sem.at[number + 2], n_dev)
+
+    def finish_coarse(sums, number):
+        coarse_wait(sums, bulk_recv, number)
+        totals = [add_slots(sums.at[index], n_dev) for index in range(3)]
+        totals = jnp.concatenate(
+            [totals[0] * low_wall, totals[1], totals[2] * high_wall]
+            + [jnp.zeros((5, LANES), jnp.float32)],
+            axis=0,
+        )
+        spread = jnp.dot(
+            totals, pick_ref[...], precision=HIGHEST, preferred_element_type=jnp.float32
+        )
+        before, here, after = (spread[:, m * LANES : (m + 1) * LANES] for m in range(3))
         node = lax.broadcasted_iota(jnp.int32, (NP, LANES), 0)
-        beside = jnp.where(node == 0, previous_lane(sol, 1), 0.0) + jnp.where(
-            node == NP - 1, next_lane(sol, 1), 0.0
-        )
-        return w_k * (sol + beside)
+        out = []
+        for value in (here + before, here, here + after):
+            left = previous_lane(value, 1)
+            right = next_lane(value, 1)
+            lines = []
+            for index in range(3):
+                row = slice(index, index + 1)
+                lines.append(
+                    w_k
+                    * (
+                        value[row]
+                        + jnp.where(node == 0, left[row], 0.0)
+                        + jnp.where(node == NP - 1, right[row], 0.0)
+                    )
+                )
+            out.append((lines[1] + lines[0], lines[1], lines[1] + lines[2]))
+        return out
 
     even = [a for a in range(NX) if abs(trans[0, a] - trans[9, a]) < abs(trans[0, a] + trans[9, a])]
     odd = [a for a in range(NX) if a not in even]
 
-    def local_solve(ext, out):
-        for pair in PAIRS:
+    def forward(ext, pairs):
+        for pair in pairs:
             parts = []
             for i in pair:
                 front = previous_lane(ext[i, pl.ds(6, 16, stride=NP), :], 1)
@@ -468,6 +565,7 @@
             work[pair[0]] = got[:, 0:LANES]
             work[pair[1]] = got[:, LANES:]
 
+    def solve_modes():
         def middle(block, carry):
             rows = pl.ds(pl.multiple_of(block * 8, 8), 8)
             vals = [work[i, rows, :] for i in range(NX)]
@@ -484,8 +582,10 @@
                 work[NX - 1 - i, rows, :] = sym - anti
             return carry
 
-        lax.fori_loop(0, KROWS // 8, middle, 0)
-        for pair in PAIRS:
+        lax.fori_loop(0, KROWS // 8 - 1, middle, 0)
+
+    def backward(out, pairs):
+        for pair in pairs:
             got = dot_split(
                 back_ref[...], jnp.concatenate([work[pair[0]], work[pair[1]]], axis=1)
             )
@@ -503,13 +603,25 @@
                 out[i, at_0, :] = top + previous_lane(bottom, 1)
                 out[i, at_7, :] = bottom + next_lane(top, 1)
 
-    def add_coarse(out, coarse):
-        for i in range(NP):
-            for j in range(NP):
-                rows = slice(8 + NP * j, 16 + NP * j)
-                out[i + 1, rows, :] = out[i + 1, rows, :] + (weights[i] * weights[j]) * coarse
-
-    def fold_field(out, i, x_buf, y_buf, c_buf):
+    def extend_and_solve(arriving, ext, own, buffers, part, sums, number, out, between):
+        arrive(arriving[6:8])
+        extend_into(ext, range(2, 8), own, *buffers)
+        forward(ext, INNER)
+        arrive(arriving[4:6])
+        arrive(arriving[0:4])
+        extend_into(ext, (0, 1, 8, 9), own, *buffers)
+        start_coarse(ext, part, sums, number)
+        forward(ext, OUTER)
+        between()
+        solve_modes()
+        backward(out, OUTER)
+
+    def send_folds(number, out, buffers):
+        copies = exchange(number, CORNERS + ALONG_X, out, QF_X, QF_Y, *buffers)
+        backward(out, INNER)
+        return copies + exchange(number, ALONG_Y, out, QF_X, QF_Y, *buffers)
+
+    def fold_field(out, coarse, i, x_buf, y_buf, c_buf):
         row = out[i + 1, 8:72, :]
         low = y_buf[0, i]
         high = y_buf[1, i]
@@ -521,9 +633,14 @@
             row = row + x_buf[1, i - 6]
             low = low + c_buf[1, 0, i - 6]
             high = high + c_buf[1, 1, i - 6]
+        lines = coarse[0 if i == 0 else 2 if i == NP - 1 else 1]
+        terms = [
+            (weights[i] * weights[j]) * lines[0 if j == 0 else 2 if j == NP - 1 else 1]
+            for j in range(NP)
+        ]
         return jnp.concatenate(
             [row[0:16] + low * low_wall, row[16:48], row[48:64] + high * high_wall], axis=0
-        )
+        ) + jnp.concatenate(terms, axis=0)
 
     def operate(field, out):
         total = jnp.zeros((NP, LANES), jnp.float32)
@@ -553,14 +670,6 @@
                     total = total + result * vals[at]
         return total
 
-    def inverse_mult(i, j):
-        scale = 0.5 if i in (0, NP - 1) else 1.0
-        if j == 0:
-            return scale * (1.0 - 0.5 * low_wall)
-        if j == NP - 1:
-            return scale * (1.0 - 0.5 * high_wall)
-        return scale
-
     def product(left, right):
         total = jnp.zeros((NP, LANES), jnp.float32)
         for j in range(NP):
@@ -602,53 +711,53 @@
             rows = [rows[index] + rows[index + 1] for index in range(0, len(rows), 2)]
         return rows[0]
 
-    arrive(round_1)
-    extend_into(e0, u0, x1, y1, c1)
-    start_coarse(e0, coarse_a, 0)
-    local_solve(e0, s0)
-    add_coarse(s0, finish_coarse(coarse_a, 0))
-    round_2 = exchange(1, s0, QF_X, QF_Y, x2, y2, c2)
+    extend_and_solve(
+        round_1, e0, u0, (x1, y1, c1), part_a, sums_a, 0, s0, lambda: None
+    )
+    round_2 = send_folds(1, s0, (x2, y2, c2))
     arrive(round_2)
+    coarse = finish_coarse(sums_a, 0)
     for i in range(NP):
-        z0[i] = fold_field(s0, i, x2, y2, c2)
+        z0[i] = fold_field(s0, coarse, i, x2, y2, c2)
 
     delta_part = operate(z0, u1)
     assemble_z(u1)
-    round_3 = exchange(2, u1, EQ_X, EQ_Y, x3, y3, c3)
+    round_3 = exchange(2, SIDES, u1, EQ_X, EQ_Y, x3, y3, c3)
     gamma_part = product(from_ext(e0), from_field(z0))
     dots_a[dev] = pack_dots([gamma_part, delta_part])
-    spread_row(dots_a, 2, True)
-    arrive(round_3)
-    extend_into(e1, u1, x3, y3, c3)
-
-    start_coarse(e1, coarse_b, 1)
-    local_solve(e1, s1)
-    add_coarse(s1, finish_coarse(coarse_b, 1))
-    round_4 = exchange(3, s1, QF_X, QF_Y, x4, y4, c4)
-    bulk_wait(dots_a, bulk_recv.at[2], n_dev)
-    dots_b[grp] = add_slots(dots_a, n_dev)
-    spread_row(dots_b, 3, False)
-    bulk_wait(dots_b, bulk_recv.at[3], n_grp)
+    spread_row(dots_a, 6, True)
+
+    def second_half():
+        bulk_wait(dots_a, bulk_recv.at[6], n_dev - 1)
+        dots_b[grp] = add_slots(dots_a, n_dev)
+        spread_row(dots_b, 7, False)
+
+    extend_and_solve(
+        round_3, e1, u1, (x3, y3, c3), part_b, sums_b, 3, s1, second_half
+    )
+    round_4 = send_folds(3, s1, (x4, y4, c4))
+    bulk_wait(dots_b, bulk_recv.at[7], n_grp - 1)
     first_dots = add_slots(dots_b, n_grp)
     gamma_0 = unpack_dot(first_dots, 0)
     delta_0 = unpack_dot(first_dots, 1)
     alpha_0 = gamma_0 / delta_0
-    arrive(round_4)
-    for i in range(NP):
-        z1[i] = z0[i] - alpha_0 * fold_field(s1, i, x4, y4, c4)
-
-    zeta_part = operate(z1, u2)
-    assemble_z(u2)
-    round_5 = exchange(4, u2, Q_X, Q_Y, x5, y5, c5)
     for i in range(NP):
         res_ref[i] = e0[i + 1, 8:72, :] - alpha_0 * e1[i + 1, 8:72, :]
+    arrive(round_4)
+    coarse = finish_coarse(sums_b, 3)
+    for i in range(NP):
+        z1[i] = z0[i] - alpha_0 * fold_field(s1, coarse, i, x4, y4, c4)
+
     gamma_part = product(from_field(res_ref), from_field(z1))
     eta_part = product(from_ext(e1), from_field(z1))
+    zeta_part = operate(z1, u2)
     dots_c[dev] = pack_dots([gamma_part, eta_part, zeta_part])
-    spread_row(dots_c, 4, True)
-    bulk_wait(dots_c, bulk_recv.at[4], n_dev)
+    spread_row(dots_c, 8, True)
+    assemble_z(u2)
+    round_5 = exchange(4, SIDES, u2, Q_X, Q_Y, x5, y5, c5)
+    bulk_wait(dots_c, bulk_recv.at[8], n_dev - 1)
     dots_d[grp] = add_slots(dots_c, n_dev)
-    spread_row(dots_d, 5, False)
+    spread_row(dots_d, 9, False)
     arrive(round_5)
     for i in range(NP):
         row = u2[i]
@@ -665,7 +774,7 @@
         e0[i, 0:8, :] = row[0:8] + low * low_wall
         e0[i, 8:56, :] = row[8:56]
         e0[i, 56:64, :] = row[56:64] + high * high_wall
-    bulk_wait(dots_d, bulk_recv.at[5], n_grp)
+    bulk_wait(dots_d, bulk_recv.at[9], n_grp - 1)
     last_dots = add_slots(dots_d, n_grp)
     gamma_1 = unpack_dot(last_dots, 0)
     eta = unpack_dot(last_dots, 1)
@@ -680,17 +789,15 @@
     for copies in (round_1, round_2, round_3, round_4, round_5):
         for copy in copies:
             copy.wait_send()
-    for number, (buf, count) in enumerate(
-        (
-            (coarse_a, n_dev),
-            (coarse_b, n_dev),
-            (dots_a, n_dev),
-            (dots_b, n_grp),
-            (dots_c, n_dev),
-            (dots_d, n_grp),
-        )
+    coarse_wait(sums_a, bulk_send, 0)
+    coarse_wait(sums_b, bulk_send, 3)
+    for number, buf, count in (
+        (6, dots_a, n_dev),
+        (7, dots_b, n_grp),
+        (8, dots_c, n_dev),
+        (9, dots_d, n_grp),
     ):
-        bulk_wait(buf, bulk_send.at[number], count)
+        bulk_wait(buf, bulk_send.at[number], count - 1)
 
 
 def local(n_grp, n_dev, forcing, coefficient, coarse_inverse):
@@ -710,33 +817,45 @@
     modes = pltpu.VMEM((NX, KROWS, LANES), jnp.float32)
     along_dev = pltpu.VMEM((n_dev, 1, LANES), jnp.float32)
     along_grp = pltpu.VMEM((n_grp, 1, LANES), jnp.float32)
+    three_groups = pltpu.VMEM((3, n_dev, 1, LANES), jnp.float32)
     out = jax.ShapeDtypeStruct(field, jnp.float32)
     columns = n_dev * coarse_inverse.shape[0]
     solved, residual = pl.pallas_call(
         functools.partial(kernel, n_grp, n_dev),
         out_shape=(out, out),
-        in_specs=[vmem] * 7,
+        in_specs=[pl.BlockSpec(memory_space=pltpu.HBM)] * 4,
         out_specs=(vmem, vmem),
         scratch_shapes=[
+            pltpu.VMEM((1, LANES), jnp.float32),
+            pltpu.VMEM(coarse_inverse[:, :columns].shape, jnp.float32),
+            pltpu.VMEM((TABLE_ROWS, LANES), jnp.float32),
+            pltpu.VMEM((2 * KROWS, 2 * LANES), jnp.bfloat16),
+            pltpu.VMEM((2 * KROWS, 2 * LANES), jnp.bfloat16),
+            pltpu.VMEM((128, LANES), jnp.bfloat16),
+            pltpu.VMEM((LANES, 3 * LANES), jnp.float32),
             full, full, full, ext, ext, ext, ext, full, full, modes, modes,
             *buffers(2), *buffers(2), *buffers(2), *buffers(2), *buffers(1),
-            along_dev, along_dev, along_dev, along_grp, along_dev, along_grp,
+            along_dev, along_dev, three_groups, three_groups,
+            along_dev, along_grp, along_dev, along_grp,
+            pltpu.SemaphoreType.DMA((4,)),
             pltpu.SemaphoreType.DMA((5, 8)),
             pltpu.SemaphoreType.DMA((5, 8)),
-            pltpu.SemaphoreType.DMA((6,)),
-            pltpu.SemaphoreType.DMA((6,)),
+            pltpu.SemaphoreType.DMA((10,)),
+            pltpu.SemaphoreType.DMA((10,)),
         ],
         compiler_params=pltpu.CompilerParams(
             collective_id=0, has_side_effects=True, vmem_limit_bytes=40 * 1024 * 1024
         ),
     )(
-        forcing.reshape(field),
-        coefficient.reshape(1, LANES),
-        coarse_inverse[:, :columns],
-        jnp.asarray(tabs["table"]),
-        jnp.asarray(tabs["forward"]),
-        jnp.asarray(tabs["back"]),
-        jnp.asarray(tabs["plane"]),
+        *(
+            pltpu.with_memory_space_constraint(array, pltpu.HBM)
+            for array in (
+                forcing.reshape(field),
+                coefficient.reshape(1, LANES),
+                coarse_inverse[:, :columns],
+                jnp.asarray(tabs["table"]),
+            )
+        )
     )
     return solved.reshape(forcing.shape), residual.reshape(forcing.shape)
 

time: 70.1 us -> 56.5 us (0.81)
  Pallas kernels: 61.8 us -> 54.3 us
  local copies, waits for them, and re-layouts: 7.3 us -> 1.41 us
    pallas_call x1, Pallas kernels: 61.8 us -> 54.3 us  [local(): pl.pallas_call(functools.partial(kernel, n_grp, n_dev), out_shape=(out, o...]
    unnamed x16 -> x2, local copies, waits for them, and re-layouts: 7.3 us -> 1.41 us
where the time goes in v2:
time: 56.5 us; the launch traced here: 56.3 us
  Pallas kernels  54.3 us (96%)
  local copies, waits for them, and re-layouts  1.41 us (2%)
  between operations  0.64 us (1%)
    pallas_call x1, Pallas kernels, local(): pl.pallas_call(functools.partial(kernel, n_grp, n_dev), out_shape=(out, o...  54.3 us
    unnamed x2, local copies, waits for them, and re-layouts  1.41 us

profile of v2, /device:TPU:1, one launch (start us, length us, event | category | flops | bytes accessed | tf_op | source)
XLA Modules:
  0.0 56.3 jit_solution(10331550533203330322)
XLA Ops:
  0.6 54.3 %shard_map.59 = (f32[8,64,128]{2,1,0:T(8,128)S(1)}, f32[8,64,128]{2,1,0:T(8,128)S(1)}) custom-call(f32[8,64,128]{2,1,0:T(8,128)} %bitcast.10, f32[1,128]{1,0:T(1,128)} %bitcast.11, f32[32,1024]{1,0:T(8,128)} %rows_hbm.1, f32[704,128]{1,0:T(8,128)} %constant.2.clone.table_hbm), custom_call_target="tpu_custom_call" | custom-call | tf_op jit(solution)/shard_map/pallas_call | solution.py:823
  54.9 0.7 %copy.10 = f32[8,8,8,1,1,128]{5,4,3,2,1,0:T(1,128)} copy(f32[8,8,8,1,1,128]{5,4,3,2,1,0:T(1,128)S(1)} %bitcast.9) | data formatting | bytes 524288
  55.6 0.7 %copy.11 = f32[8,8,8,1,1,128]{5,4,3,2,1,0:T(1,128)} copy(f32[8,8,8,1,1,128]{5,4,3,2,1,0:T(1,128)S(1)} %bitcast.8) | data formatting | bytes 524288

commit v3 on v2

--- a/solution.py
+++ b/solution.py
@@ -243,8 +243,15 @@
     coef_hbm,
     rows_hbm,
     table_hbm,
-    sol_ref,
+    z0,
+    z1,
     res_ref,
+    q0,
+    image_ref,
+    step_z0,
+    step_z1,
+    step_q0,
+    step_s0,
     coef_ref,
     rows_ref,
     table_ref,
@@ -252,6 +259,7 @@
     back_ref,
     plane_ref,
     pick_ref,
+    place_ref,
     u0,
     u1,
     u2,
@@ -259,8 +267,6 @@
     e1,
     s0,
     s1,
-    z0,
-    z1,
     work,
     inv_ref,
     x1,
@@ -282,7 +288,7 @@
     part_b,
     sums_a,
     sums_b,
-    dots_a,
+    near_rows,
     dots_b,
     dots_c,
     dots_d,
@@ -291,6 +297,8 @@
     recv_sem,
     bulk_send,
     bulk_recv,
+    near_sem,
+    far_sem,
 ):
     tabs = constants()
     weights = tabs["weights"]
@@ -320,29 +328,26 @@
     for load in loads:
         load.start()
 
+    n_x = 4
+    n_z = n_dev // n_x
+    my_x = dev // n_z
+    my_z = lax.rem(dev, n_z)
+
+    def place_at(step_x, step_z):
+        return lax.rem(my_x + step_x, n_x) * n_z + lax.rem(my_z + step_z, n_z)
+
+    def signal(sem, where):
+        pl.semaphore_signal(
+            sem, inc=1, device_id=where, device_id_type=pl.DeviceIdType.MESH
+        )
+
     barrier = pltpu.get_barrier_semaphore()
-
-    def greet_dev(step, carry):
-        pl.semaphore_signal(
-            barrier, inc=1, device_id=(grp, lax.rem(dev + step, n_dev)),
-            device_id_type=pl.DeviceIdType.MESH,
-        )
-        return carry
-
-    def greet_grp(step, carry):
-        pl.semaphore_signal(
-            barrier, inc=1, device_id=(lax.rem(grp + step, n_grp), dev),
-            device_id_type=pl.DeviceIdType.MESH,
-        )
-        return carry
-
-    lax.fori_loop(1, n_dev, greet_dev, 0)
-    lax.fori_loop(1, n_grp, greet_grp, 0)
-    for dx, dy in CORNERS:
-        pl.semaphore_signal(
-            barrier, inc=1, device_id=(grp_at(dy), dev_at(dx)),
-            device_id_type=pl.DeviceIdType.MESH,
-        )
+    greeted = [(grp_at(dy), dev_at(dx)) for dx, dy in SIDES]
+    greeted += [(grp, place_at(0, step)) for step in range(1, n_z)]
+    greeted += [(grp, place_at(step, 0)) for step in range(1, n_x)]
+    greeted += [(grp_at(step), dev) for step in range(2, n_grp, 2)]
+    for where in greeted:
+        signal(barrier, where)
 
     def exchange(number, sides, source, x_ranges, y_ranges, x_buf, y_buf, c_buf):
         copies = []
@@ -383,6 +388,10 @@
             device_id_type=pl.DeviceIdType.MESH,
         ).start()
 
+    def from_middle(turn, count):
+        half = (turn + 1) // 2
+        return count // 2 + half * (1 - 2 * lax.rem(turn, 2))
+
     def spread_row(buf, number, along_dev):
         count = n_dev if along_dev else n_grp
         me = dev if along_dev else grp
@@ -410,8 +419,10 @@
 
     loads[0].wait()
     assemble_z(u0)
-    pl.semaphore_wait(barrier, n_dev - 1 + n_grp - 1 + 4)
+    pl.semaphore_wait(barrier, len(greeted))
     round_1 = exchange(0, SIDES, u0, EQ_X, EQ_Y, x1, y1, c1)
+    for step in range(1, n_x):
+        signal(near_sem, (grp, place_at(step, 0)))
     for load in loads[1:]:
         load.wait()
 
@@ -432,12 +443,20 @@
     elem = lax.broadcasted_iota(jnp.int32, (LANES, LANES), 1)
     for index in range(3):
         block = lax.rem(dev + index + 3, 4)
+        place_ref[index * LANES : (index + 1) * LANES, :] = jnp.where(
+            elem == block * 32 + lax.shift_right_logical(place, 2), 1.0, 0.0
+        ).astype(jnp.float32)
+    for index in range(3):
+        block = lax.rem(dev + index + 3, 4)
         pick_ref[:, index * LANES : (index + 1) * LANES] = jnp.where(
             place == block * 32 + lax.shift_right_logical(elem, 2), 1.0, 0.0
         ).astype(jnp.float32)
     lam_rows = table_ref[0:KROWS, :]
     for a in range(NX):
         inv_ref[a] = 1.0 / (coef * (lam_rows + eigen[a]) + MASS_SHIFT)
+    pl.semaphore_wait(near_sem, n_x - 1)
+    for dx, dy in ALONG_Y:
+        signal(far_sem, (grp_at(dy), dev_at(dx)))
     zero_rows = jnp.zeros((128 - 80, LANES), jnp.float32)
     for i in range(NX):
         e0[i, 80:128, :] = zero_rows
@@ -501,19 +520,130 @@
         up = grp_at(1)
         down = grp_at(-1)
 
-        def send(step, carry):
-            other = lax.rem(dev + step, n_dev)
+        def send(turn, own):
+            other = place_at(from_middle(lax.rem(turn, n_x), n_x), from_middle(turn // n_x, n_z))
             send_row(part.at[other], sums.at[0, dev], number, (up, other))
             send_row(part.at[other], sums.at[2, dev], number + 2, (down, other))
+            if own:
+                send_row(part.at[other], sums.at[1, dev], number + 1, (grp, other))
+
+        def body(turn, carry):
+            send(turn, True)
             return carry
 
-        def send_own(step, carry):
-            other = lax.rem(dev + step, n_dev)
-            send_row(part.at[other], sums.at[1, dev], number + 1, (grp, other))
-            return send(step, carry)
-
-        lax.fori_loop(1, n_dev, send_own, 0)
-        send(0, 0)
+        lax.fori_loop(0, n_dev - 1, body, 0)
+        send(n_dev - 1, False)
+
+    def send_shares(part, sums, number):
+        up = grp_at(1)
+        down = grp_at(-1)
+
+        def send(turn, own):
+            other = place_at(from_middle(lax.rem(turn, n_x), n_x), from_middle(turn // n_x, n_z))
+            send_row(part.at[2], sums.at[0, dev], number, (up, other))
+            send_row(part.at[0], sums.at[2, dev], number + 2, (down, other))
+            if own:
+                send_row(part.at[1], sums.at[1, dev], number + 1, (grp, other))
+
+        def body(turn, carry):
+            send(turn, True)
+            return carry
+
+        lax.fori_loop(0, n_dev - 1, body, 0)
+        send(n_dev - 1, False)
+
+    def start_early(field, part, sums, number, dots):
+        totals = []
+        lines = {-1: [], 0: [], 1: []}
+        for j in range(NP):
+            rows = slice(NP * j, NP * j + NP)
+            lines[0].append(combine(weights, [field[i, rows, :] for i in range(NP)]))
+            lines[1].append(weights[0] * field[NP - 1, rows, :])
+            lines[-1].append(weights[NP - 1] * field[0, rows, :])
+        for step in (-1, 0, 1):
+            line = lines[step]
+            three = (weights[NP - 1] * line[0], combine(weights, line), weights[0] * line[NP - 1])
+            totals.append(
+                jnp.concatenate(
+                    [jnp.sum(value * w_k, axis=0, keepdims=True) for value in three]
+                    + [jnp.zeros((5, LANES), jnp.float32)],
+                    axis=0,
+                )
+            )
+        rows = jnp.dot(
+            jnp.concatenate(totals, axis=1),
+            place_ref[...],
+            precision=HIGHEST,
+            preferred_element_type=jnp.float32,
+        )
+        own = rows[1:2]
+        free = lax.rem(dev + 2, 4) * 32
+        for index, total in enumerate(dots):
+            first = free + 16 * index
+            row = lane_fold(jnp.sum(total, axis=0, keepdims=True))
+            row = row + pltpu.roll(row, 16, 1)
+            own = own + jnp.where((lane >= first) & (lane < first + 16), row, 0.0)
+        part[0] = rows[0:1]
+        part[1] = own
+        part[2] = rows[2:3]
+        sums[1, dev] = own
+        send_shares(part, sums, number)
+
+    def early_dots(sums, number):
+        bulk_wait(sums.at[1], bulk_recv.at[number + 1], n_dev - 1)
+        total = None
+        for quarter in range(4):
+            rows = [sums[1, index] for index in range(quarter, n_dev, 4)]
+            row = functools.reduce(lambda a, b: a + b, rows)
+            first = (quarter + 2) % 4 * 32
+            row = jnp.where((lane >= first) & (lane < first + 32), row, 0.0)
+            total = row if total is None else total + row
+        return lane_fold(total)
+
+    def spread_solution(sums, number):
+        bulk_wait(sums.at[0], bulk_recv.at[number], n_dev)
+        bulk_wait(sums.at[2], bulk_recv.at[number + 2], n_dev)
+        rows = [
+            sums[1, index] + (sums[0, index] * low_wall + sums[2, index] * high_wall)
+            for index in range(n_dev)
+        ]
+        total = None
+        for m in range(n_dev // 4):
+            row = (
+                jnp.where(lane < 64, rows[4 * m], 0.0)
+                + jnp.where(lane < 96, rows[4 * m + 1], 0.0)
+                + jnp.where(lane >= 32, rows[4 * m + 2], 0.0)
+                + jnp.where(lane >= 64, rows[4 * m + 3], 0.0)
+                + jnp.where(lane >= 96, rows[(4 * m + 4) % n_dev], 0.0)
+                + jnp.where(lane < 32, rows[4 * m - 1], 0.0)
+            )
+            term = rows_ref[:, m * LANES : (m + 1) * LANES] * row
+            total = term if total is None else total + term
+        sums_q = jnp.sum(total, axis=1, keepdims=True)
+        unknown = lax.broadcasted_iota(jnp.int32, (32, LANES), 0)
+        elem = lax.broadcasted_iota(jnp.int32, (32, LANES), 1)
+        mine = lax.shift_right_logical(elem, 2) == unknown
+        near_rows[4] = jnp.sum(jnp.where(mine, sums_q, 0.0), axis=0, keepdims=True)
+        for dx, dy in SIDES:
+            send_row(
+                near_rows.at[4],
+                near_rows.at[3 * (1 - dy) + 1 - dx],
+                6,
+                (grp_at(dy), dev_at(dx)),
+            )
+
+    def near_lines():
+        bulk_wait(near_rows, bulk_recv.at[6], 8)
+        sides = []
+        for index in range(3):
+            sides.append(
+                jnp.concatenate(
+                    [near_rows[index] * low_wall, near_rows[3 + index], near_rows[6 + index] * high_wall]
+                    + [jnp.zeros((5, LANES), jnp.float32)],
+                    axis=0,
+                )
+            )
+        return coarse_lines(*sides)
 
     def coarse_wait(sums, sem, number):
         bulk_wait(sums.at[0], sem.at[number], n_dev)
@@ -531,7 +661,9 @@
         spread = jnp.dot(
             totals, pick_ref[...], precision=HIGHEST, preferred_element_type=jnp.float32
         )
-        before, here, after = (spread[:, m * LANES : (m + 1) * LANES] for m in range(3))
+        return coarse_lines(*(spread[:, m * LANES : (m + 1) * LANES] for m in range(3)))
+
+    def coarse_lines(before, here, after):
         node = lax.broadcasted_iota(jnp.int32, (NP, LANES), 0)
         out = []
         for value in (here + before, here, here + after):
@@ -603,16 +735,15 @@
                 out[i, at_0, :] = top + previous_lane(bottom, 1)
                 out[i, at_7, :] = bottom + next_lane(top, 1)
 
-    def extend_and_solve(arriving, ext, own, buffers, part, sums, number, out, between):
+    def extend_and_solve(arriving, ext, own, buffers, out, between):
         arrive(arriving[6:8])
         extend_into(ext, range(2, 8), own, *buffers)
         forward(ext, INNER)
         arrive(arriving[4:6])
         arrive(arriving[0:4])
         extend_into(ext, (0, 1, 8, 9), own, *buffers)
-        start_coarse(ext, part, sums, number)
+        between()
         forward(ext, OUTER)
-        between()
         solve_modes()
         backward(out, OUTER)
 
@@ -701,8 +832,8 @@
             packed = row if packed is None else packed + row
         return packed
 
-    def unpack_dot(row, index):
-        mine = (lane >= 32 * index) & (lane < 32 * index + 32)
+    def unpack_dot(row, index, width):
+        mine = (lane >= width * index) & (lane < width * index + width)
         return jnp.sum(jnp.where(mine, row, 0.0), axis=1, keepdims=True)
 
     def add_slots(buf, count):
@@ -711,8 +842,9 @@
             rows = [rows[index] + rows[index + 1] for index in range(0, len(rows), 2)]
         return rows[0]
 
+    pl.semaphore_wait(far_sem, 2)
     extend_and_solve(
-        round_1, e0, u0, (x1, y1, c1), part_a, sums_a, 0, s0, lambda: None
+        round_1, e0, u0, (x1, y1, c1), s0, lambda: start_coarse(e0, part_a, sums_a, 0)
     )
     round_2 = send_folds(1, s0, (x2, y2, c2))
     arrive(round_2)
@@ -724,34 +856,37 @@
     assemble_z(u1)
     round_3 = exchange(2, SIDES, u1, EQ_X, EQ_Y, x3, y3, c3)
     gamma_part = product(from_ext(e0), from_field(z0))
-    dots_a[dev] = pack_dots([gamma_part, delta_part])
-    spread_row(dots_a, 6, True)
-
-    def second_half():
-        bulk_wait(dots_a, bulk_recv.at[6], n_dev - 1)
-        dots_b[grp] = add_slots(dots_a, n_dev)
-        spread_row(dots_b, 7, False)
-
-    extend_and_solve(
-        round_3, e1, u1, (x3, y3, c3), part_b, sums_b, 3, s1, second_half
-    )
+    start_early(u1, part_b, sums_b, 3, (gamma_part, delta_part))
+
+    extend_and_solve(round_3, e1, u1, (x3, y3, c3), s1, lambda: None)
     round_4 = send_folds(3, s1, (x4, y4, c4))
+    dots_b[grp] = early_dots(sums_b, 3)
+    spread_row(dots_b, 7, False)
+    spread_solution(sums_b, 3)
+    for i in range(NP):
+        q0[i] = e1[i + 1, 8:72, :]
+    arrive(round_4)
+    coarse = near_lines()
+    for i in range(NP):
+        z1[i] = fold_field(s1, coarse, i, x4, y4, c4)
+
+    operate(z1, u2)
     bulk_wait(dots_b, bulk_recv.at[7], n_grp - 1)
     first_dots = add_slots(dots_b, n_grp)
-    gamma_0 = unpack_dot(first_dots, 0)
-    delta_0 = unpack_dot(first_dots, 1)
+    gamma_0 = unpack_dot(first_dots, 0, 16)
+    delta_0 = unpack_dot(first_dots, 1, 16)
     alpha_0 = gamma_0 / delta_0
     for i in range(NP):
-        res_ref[i] = e0[i + 1, 8:72, :] - alpha_0 * e1[i + 1, 8:72, :]
-    arrive(round_4)
-    coarse = finish_coarse(sums_b, 3)
+        z1[i] = z0[i] - alpha_0 * z1[i]
+        res_ref[i] = e0[i + 1, 8:72, :] - alpha_0 * q0[i]
+    gamma_part = product(from_field(res_ref), from_field(z1))
+    eta_part = product(from_field(q0), from_field(z1))
+    theta_part = None
     for i in range(NP):
-        z1[i] = z0[i] - alpha_0 * fold_field(s1, coarse, i, x4, y4, c4)
-
-    gamma_part = product(from_field(res_ref), from_field(z1))
-    eta_part = product(from_ext(e1), from_field(z1))
-    zeta_part = operate(z1, u2)
-    dots_c[dev] = pack_dots([gamma_part, eta_part, zeta_part])
+        for j in range(NP):
+            term = from_field(z1)(i, j) * from_field(u2)(i, j)
+            theta_part = term if theta_part is None else theta_part + term
+    dots_c[dev] = pack_dots([gamma_part, eta_part, theta_part])
     spread_row(dots_c, 8, True)
     assemble_z(u2)
     round_5 = exchange(4, SIDES, u2, Q_X, Q_Y, x5, y5, c5)
@@ -771,20 +906,23 @@
             row = row + x5[1, 0]
             low = low + c5[1, 0, 0]
             high = high + c5[1, 1, 0]
-        e0[i, 0:8, :] = row[0:8] + low * low_wall
-        e0[i, 8:56, :] = row[8:56]
-        e0[i, 56:64, :] = row[56:64] + high * high_wall
+        image_ref[i, 0:8, :] = row[0:8] + low * low_wall
+        image_ref[i, 8:56, :] = row[8:56]
+        image_ref[i, 56:64, :] = row[56:64] + high * high_wall
     bulk_wait(dots_d, bulk_recv.at[9], n_grp - 1)
     last_dots = add_slots(dots_d, n_grp)
-    gamma_1 = unpack_dot(last_dots, 0)
-    eta = unpack_dot(last_dots, 1)
-    zeta = unpack_dot(last_dots, 2)
+    gamma_1 = unpack_dot(last_dots, 0, 32)
+    eta = unpack_dot(last_dots, 1, 32)
+    zeta = eta - alpha_0 * unpack_dot(last_dots, 2, 32)
     beta = gamma_1 / gamma_0
     alpha_1 = gamma_1 / (zeta + beta * (2.0 * eta + beta * delta_0))
-    scale_0 = alpha_0 + alpha_1 * beta
-    for i in range(NP):
-        sol_ref[i] = scale_0 * z0[i] + alpha_1 * z1[i]
-        res_ref[i] = res_ref[i] - alpha_1 * (e0[i, 0:64, :] + beta * e1[i + 1, 8:72, :])
+    for ref, value in (
+        (step_z0, alpha_0 + alpha_1 * beta),
+        (step_z1, alpha_1),
+        (step_q0, alpha_1 * (1.0 + beta)),
+        (step_s0, -alpha_1 * alpha_0),
+    ):
+        ref[...] = jnp.broadcast_to(value, (1, LANES))
 
     for copies in (round_1, round_2, round_3, round_4, round_5):
         for copy in copies:
@@ -792,7 +930,7 @@
     coarse_wait(sums_a, bulk_send, 0)
     coarse_wait(sums_b, bulk_send, 3)
     for number, buf, count in (
-        (6, dots_a, n_dev),
+        (6, near_rows, 9),
         (7, dots_b, n_grp),
         (8, dots_c, n_dev),
         (9, dots_d, n_grp),
@@ -817,14 +955,17 @@
     modes = pltpu.VMEM((NX, KROWS, LANES), jnp.float32)
     along_dev = pltpu.VMEM((n_dev, 1, LANES), jnp.float32)
     along_grp = pltpu.VMEM((n_grp, 1, LANES), jnp.float32)
+    three_rows = pltpu.VMEM((3, 1, LANES), jnp.float32)
+    nine_rows = pltpu.VMEM((9, 1, LANES), jnp.float32)
     three_groups = pltpu.VMEM((3, n_dev, 1, LANES), jnp.float32)
     out = jax.ShapeDtypeStruct(field, jnp.float32)
+    step = jax.ShapeDtypeStruct((1, LANES), jnp.float32)
     columns = n_dev * coarse_inverse.shape[0]
-    solved, residual = pl.pallas_call(
+    first, second, residual, first_image, second_image, *steps = pl.pallas_call(
         functools.partial(kernel, n_grp, n_dev),
-        out_shape=(out, out),
+        out_shape=(out,) * 5 + (step,) * 4,
         in_specs=[pl.BlockSpec(memory_space=pltpu.HBM)] * 4,
-        out_specs=(vmem, vmem),
+        out_specs=(vmem,) * 9,
         scratch_shapes=[
             pltpu.VMEM((1, LANES), jnp.float32),
             pltpu.VMEM(coarse_inverse[:, :columns].shape, jnp.float32),
@@ -833,15 +974,18 @@
             pltpu.VMEM((2 * KROWS, 2 * LANES), jnp.bfloat16),
             pltpu.VMEM((128, LANES), jnp.bfloat16),
             pltpu.VMEM((LANES, 3 * LANES), jnp.float32),
-            full, full, full, ext, ext, ext, ext, full, full, modes, modes,
+            pltpu.VMEM((3 * LANES, LANES), jnp.float32),
+            full, full, full, ext, ext, ext, ext, modes, modes,
             *buffers(2), *buffers(2), *buffers(2), *buffers(2), *buffers(1),
-            along_dev, along_dev, three_groups, three_groups,
-            along_dev, along_grp, along_dev, along_grp,
+            along_dev, three_rows, three_groups, three_groups,
+            nine_rows, along_grp, along_dev, along_grp,
             pltpu.SemaphoreType.DMA((4,)),
             pltpu.SemaphoreType.DMA((5, 8)),
             pltpu.SemaphoreType.DMA((5, 8)),
             pltpu.SemaphoreType.DMA((10,)),
             pltpu.SemaphoreType.DMA((10,)),
+            pltpu.SemaphoreType.REGULAR,
+            pltpu.SemaphoreType.REGULAR,
         ],
         compiler_params=pltpu.CompilerParams(
             collective_id=0, has_side_effects=True, vmem_limit_bytes=40 * 1024 * 1024
@@ -857,6 +1001,9 @@
             )
         )
     )
+    on_z0, on_z1, on_q0, on_s0 = (value.reshape(1, 1, LANES) for value in steps)
+    solved = on_z0 * first + on_z1 * second
+    residual = residual - (on_s0 * second_image + on_q0 * first_image)
     return solved.reshape(forcing.shape), residual.reshape(forcing.shape)
 
 

time: 56.5 us -> 54.8 us (0.970)
  local copies, waits for them, and re-layouts: 1.41 us -> 0 us
  Pallas kernels: 54.3 us -> 53.1 us
  other arithmetic: 0 us -> 0.9 us
    unnamed x2 -> x0, local copies, waits for them, and re-layouts: 1.41 us -> none
    pallas_call x1, Pallas kernels: 54.3 us -> 53.1 us  [local(): pl.pallas_call(functools.partial(kernel, n_grp, n_dev), out_shape=(out,)...]
    sub x0 -> x1, other arithmetic: none -> 0.9 us  [local(): residual = residual - (on_s0 * second_image + on_q0 * first_image)]
where the time goes in v3:
time: 54.8 us; the launch traced here: 54.6 us
  Pallas kernels  53.1 us (97%)
  other arithmetic  0.9 us (2%)
  between operations  0.64 us (1%)
    pallas_call x1, Pallas kernels, local(): pl.pallas_call(functools.partial(kernel, n_grp, n_dev), out_shape=(out,)...  53.1 us

profile of v3, /device:TPU:1, one launch (start us, length us, event | category | flops | bytes accessed | tf_op | source)
XLA Modules:
  0.0 54.6 jit_solution(17432181396027123804)
XLA Ops:
  0.6 53.1 %shard_map.59 = (f32[8,64,128]{2,1,0:T(8,128)S(1)}, f32[8,64,128]{2,1,0:T(8,128)S(1)}, f32[8,64,128]{2,1,0:T(8,128)S(1)}, f32[8,64,128]{2,1,0:T(8,128)S(1)}, f32...) custom-call(f32[8,64,128]{2,1,0:T(8,128)} %bitcast.16, ...), custom_call_target="tpu_custom_call" | custom-call | tf_op jit(solution)/shard_map/pallas_call | solution.py:964
  53.7 0.9 %add_subtract_fusion = (f32[8,64,128]{2,1,0:T(8,128)}, f32[8,64,128]{2,1,0:T(8,128)}) fusion(f32[8,64,128]{2,1,0:T(8,128)S(1)} %get-tuple-element.15, f32[8,64,128]{2,1,0:T(8,128)S(1)} %get-tuple-element.19, f32[8,64,128]{2,1,0:T(8,128)S(1)} %get-tuple-element.17, f32[128]{0:T(128)S(1)} %bitcast.14, f32[128]{0:T(128)S(1)} %bitcast.15, ...), kind=kLoop, calls=%fused_computation | loop fusion | flops 458752 | bytes 1837056 | tf_op jit(solution)/shard_map/sub | solution.py:1006

commit v4 on v3

--- a/solution.py
+++ b/solution.py
@@ -325,9 +325,6 @@
             )
         )
     ]
-    for load in loads:
-        load.start()
-
     n_x = 4
     n_z = n_dev // n_x
     my_x = dev // n_z
@@ -346,7 +343,11 @@
     greeted += [(grp, place_at(0, step)) for step in range(1, n_z)]
     greeted += [(grp, place_at(step, 0)) for step in range(1, n_x)]
     greeted += [(grp_at(step), dev) for step in range(2, n_grp, 2)]
-    for where in greeted:
+    for where in greeted[:8]:
+        signal(barrier, where)
+    for load in loads:
+        load.start()
+    for where in greeted[8:]:
         signal(barrier, where)
 
     def exchange(number, sides, source, x_ranges, y_ranges, x_buf, y_buf, c_buf):
@@ -886,13 +887,13 @@
         for j in range(NP):
             term = from_field(z1)(i, j) * from_field(u2)(i, j)
             theta_part = term if theta_part is None else theta_part + term
-    dots_c[dev] = pack_dots([gamma_part, eta_part, theta_part])
-    spread_row(dots_c, 8, True)
+    dots_d[grp] = pack_dots([gamma_part, eta_part, theta_part])
+    spread_row(dots_d, 9, False)
     assemble_z(u2)
     round_5 = exchange(4, SIDES, u2, Q_X, Q_Y, x5, y5, c5)
-    bulk_wait(dots_c, bulk_recv.at[8], n_dev - 1)
-    dots_d[grp] = add_slots(dots_c, n_dev)
-    spread_row(dots_d, 9, False)
+    bulk_wait(dots_d, bulk_recv.at[9], n_grp - 1)
+    dots_c[dev] = add_slots(dots_d, n_grp)
+    spread_row(dots_c, 8, True)
     arrive(round_5)
     for i in range(NP):
         row = u2[i]
@@ -909,8 +910,8 @@
         image_ref[i, 0:8, :] = row[0:8] + low * low_wall
         image_ref[i, 8:56, :] = row[8:56]
         image_ref[i, 56:64, :] = row[56:64] + high * high_wall
-    bulk_wait(dots_d, bulk_recv.at[9], n_grp - 1)
-    last_dots = add_slots(dots_d, n_grp)
+    bulk_wait(dots_c, bulk_recv.at[8], n_dev - 1)
+    last_dots = add_slots(dots_c, n_dev)
     gamma_1 = unpack_dot(last_dots, 0, 32)
     eta = unpack_dot(last_dots, 1, 32)
     zeta = eta - alpha_0 * unpack_dot(last_dots, 2, 32)

time: 54.8 us -> 53.9 us (0.984)
  Pallas kernels: 53.1 us -> 52.2 us
    pallas_call x1, Pallas kernels: 53.1 us -> 52.2 us  [local(): pl.pallas_call(functools.partial(kernel, n_grp, n_dev), out_shape=(out,)...]
where the time goes in v4:
time: 53.9 us; the launch traced here: 53.7 us
  Pallas kernels  52.2 us (97%)
  other arithmetic  0.9 us (2%)
  between operations  0.64 us (1%)
    pallas_call x1, Pallas kernels, local(): pl.pallas_call(functools.partial(kernel, n_grp, n_dev), out_shape=(out,)...  52.2 us

profile of v4, /device:TPU:1, one launch (start us, length us, event | category | flops | bytes accessed | tf_op | source)
XLA Modules:
  0.0 53.7 jit_solution(814309666233561971)
XLA Ops:
  0.6 52.2 %shard_map.59 = (f32[8,64,128]{2,1,0:T(8,128)S(1)}, f32[8,64,128]{2,1,0:T(8,128)S(1)}, f32[8,64,128]{2,1,0:T(8,128)S(1)}, f32[8,64,128]{2,1,0:T(8,128)S(1)}, f32...) custom-call(f32[8,64,128]{2,1,0:T(8,128)} %bitcast.16, ...), custom_call_target="tpu_custom_call" | custom-call | tf_op jit(solution)/shard_map/pallas_call | solution.py:965
  52.8 0.9 %add_subtract_fusion = (f32[8,64,128]{2,1,0:T(8,128)}, f32[8,64,128]{2,1,0:T(8,128)}) fusion(f32[8,64,128]{2,1,0:T(8,128)S(1)} %get-tuple-element.15, f32[8,64,128]{2,1,0:T(8,128)S(1)} %get-tuple-element.19, f32[8,64,128]{2,1,0:T(8,128)S(1)} %get-tuple-element.17, f32[128]{0:T(128)S(1)} %bitcast.14, f32[128]{0:T(128)S(1)} %bitcast.15, ...), kind=kLoop, calls=%fused_computation | loop fusion | flops 458752 | bytes 1837056 | tf_op jit(solution)/shard_map/sub | solution.py:1007

commit v5 on v4

--- a/solution.py
+++ b/solution.py
@@ -289,6 +289,7 @@
     sums_a,
     sums_b,
     near_rows,
+    group_rows,
     dots_b,
     dots_c,
     dots_d,
@@ -518,22 +519,19 @@
             for index, row in enumerate((first, pieces[m], pieces[m], last)):
                 part[4 * m + index] = row
         sums[1, dev] = part[dev]
-        up = grp_at(1)
-        down = grp_at(-1)
-
-        def send(turn, own):
+
+        def body(turn, carry):
             other = place_at(from_middle(lax.rem(turn, n_x), n_x), from_middle(turn // n_x, n_z))
-            send_row(part.at[other], sums.at[0, dev], number, (up, other))
-            send_row(part.at[other], sums.at[2, dev], number + 2, (down, other))
-            if own:
-                send_row(part.at[other], sums.at[1, dev], number + 1, (grp, other))
-
-        def body(turn, carry):
-            send(turn, True)
+            send_row(part.at[other], sums.at[1, dev], number + 1, (grp, other))
             return carry
 
         lax.fori_loop(0, n_dev - 1, body, 0)
-        send(n_dev - 1, False)
+
+    def pass_coarse(sums, number):
+        bulk_wait(sums.at[1], bulk_recv.at[number + 1], n_dev - 1)
+        group_rows[1] = add_slots(sums.at[1], n_dev)
+        send_row(group_rows.at[1], group_rows.at[0], number, (grp_at(1), dev))
+        send_row(group_rows.at[1], group_rows.at[2], number + 2, (grp_at(-1), dev))
 
     def send_shares(part, sums, number):
         up = grp_at(1)
@@ -652,8 +650,9 @@
         bulk_wait(sums.at[2], sem.at[number + 2], n_dev)
 
     def finish_coarse(sums, number):
-        coarse_wait(sums, bulk_recv, number)
-        totals = [add_slots(sums.at[index], n_dev) for index in range(3)]
+        bulk_wait(group_rows, bulk_recv.at[number], 1)
+        bulk_wait(group_rows, bulk_recv.at[number + 2], 1)
+        totals = [group_rows[index] for index in range(3)]
         totals = jnp.concatenate(
             [totals[0] * low_wall, totals[1], totals[2] * high_wall]
             + [jnp.zeros((5, LANES), jnp.float32)],
@@ -848,6 +847,7 @@
         round_1, e0, u0, (x1, y1, c1), s0, lambda: start_coarse(e0, part_a, sums_a, 0)
     )
     round_2 = send_folds(1, s0, (x2, y2, c2))
+    pass_coarse(sums_a, 0)
     arrive(round_2)
     coarse = finish_coarse(sums_a, 0)
     for i in range(NP):
@@ -928,7 +928,9 @@
     for copies in (round_1, round_2, round_3, round_4, round_5):
         for copy in copies:
             copy.wait_send()
-    coarse_wait(sums_a, bulk_send, 0)
+    bulk_wait(group_rows, bulk_send.at[0], 1)
+    bulk_wait(sums_a.at[1], bulk_send.at[1], n_dev - 1)
+    bulk_wait(group_rows, bulk_send.at[2], 1)
     coarse_wait(sums_b, bulk_send, 3)
     for number, buf, count in (
         (6, near_rows, 9),
@@ -979,7 +981,7 @@
             full, full, full, ext, ext, ext, ext, modes, modes,
             *buffers(2), *buffers(2), *buffers(2), *buffers(2), *buffers(1),
             along_dev, three_rows, three_groups, three_groups,
-            nine_rows, along_grp, along_dev, along_grp,
+            nine_rows, three_rows, along_grp, along_dev, along_grp,
             pltpu.SemaphoreType.DMA((4,)),
             pltpu.SemaphoreType.DMA((5, 8)),
             pltpu.SemaphoreType.DMA((5, 8)),

time: 53.9 us -> 54.2 us (level)
  no operation moved by 1% of the time
where the time goes in v5:
time: 54.2 us; the launch traced here: 54.1 us
  Pallas kernels  52.5 us (97%)
  other arithmetic  0.9 us (2%)
  between operations  0.64 us (1%)
    pallas_call x1, Pallas kernels, local(): pl.pallas_call(functools.partial(kernel, n_grp, n_dev), out_shape=(out,)...  52.5 us

profile of v5, /device:TPU:1, one launch (start us, length us, event | category | flops | bytes accessed | tf_op | source)
XLA Modules:
  0.0 54.1 jit_solution(2678346741770901982)
XLA Ops:
  0.6 52.5 %shard_map.59 = (f32[8,64,128]{2,1,0:T(8,128)S(1)}, f32[8,64,128]{2,1,0:T(8,128)S(1)}, f32[8,64,128]{2,1,0:T(8,128)S(1)}, f32[8,64,128]{2,1,0:T(8,128)S(1)}, f32...) custom-call(f32[8,64,128]{2,1,0:T(8,128)} %bitcast.16, ...), custom_call_target="tpu_custom_call" | custom-call | tf_op jit(solution)/shard_map/pallas_call | solution.py:967
  53.2 0.9 %add_subtract_fusion = (f32[8,64,128]{2,1,0:T(8,128)}, f32[8,64,128]{2,1,0:T(8,128)}) fusion(f32[8,64,128]{2,1,0:T(8,128)S(1)} %get-tuple-element.15, f32[8,64,128]{2,1,0:T(8,128)S(1)} %get-tuple-element.19, f32[8,64,128]{2,1,0:T(8,128)S(1)} %get-tuple-element.17, f32[128]{0:T(128)S(1)} %bitcast.14, f32[128]{0:T(128)S(1)} %bitcast.15, ...), kind=kLoop, calls=%fused_computation | loop fusion | flops 458752 | bytes 1837056 | tf_op jit(solution)/shard_map/sub | solution.py:1009
